TPU v7x, 32 devices: a whole 2x2x4 slice. The times are simulated.
32 devices in a mesh: dp: 8 (over y, x, core), prefix: 4 (over z).
Axes of the slice: x: 2, y: 2, z: 4, core: 2. Of those that a mesh axis runs over, the one named last changes fastest.
Arguments:
- hidden_in: bfloat16 [24, 1024, 1024], P('dp'), may hold values from -6 to 6
- cotangent: bfloat16 [24, 1024, 1024], P('dp'), may hold values from -6 to 6
- segment_ids: int32 [24, 1024], P('dp'), may hold values from 0 to 7, never falling along the last dimension, each value on 1 to 512 neighbouring positions
- key_mask: int32 [24, 1024], P('dp'), may hold values 0 or 1
- prefix_keys: bfloat16 [96, 1024], P('prefix'), may hold values from -6 to 6
- prefix_values: bfloat16 [96, 1024], P('prefix'), may hold values from -6 to 6
- w_query: bfloat16 [1024, 1024], P('dp', 'prefix'), may hold values from -0.1875 to 0.1875
- b_query: float32 [1024], P('prefix'), may hold values from -3 to 3
- w_key: bfloat16 [1024, 1024], P('dp', 'prefix'), may hold values from -0.1875 to 0.1875
- b_key: float32 [1024], P('prefix'), may hold values from -3 to 3
- w_value: bfloat16 [1024, 1024], P('dp', 'prefix'), may hold values from -0.1875 to 0.1875
- b_value: float32 [1024], P('prefix'), may hold values from -3 to 3
- w_attn_out: bfloat16 [1024, 1024], P('prefix', 'dp'), may hold values from -1 to 1
- b_attn_out: float32 [1024], replicated, may hold values from -3 to 3
- gain_attn: float32 [1024], replicated, may hold values from 0.1 to 1.9
- shift_attn: float32 [1024], replicated, may hold values from -3 to 3
- w_ffn_in: bfloat16 [1024, 4096], P('dp', 'prefix'), may hold values from -0.1875 to 0.1875
- b_ffn_in: float32 [4096], P('prefix'), may hold values from -3 to 3
- w_ffn_out: bfloat16 [4096, 1024], P('prefix', 'dp'), may hold values from -0.09375 to 0.09375
- b_ffn_out: float32 [1024], replicated, may hold values from -3 to 3
- gain_ffn: float32 [1024], replicated, may hold values from 0.1 to 1.9
- shift_ffn: float32 [1024], replicated, may hold values from -3 to 3
Outputs:
- output: bfloat16 [24, 1024, 1024], P('dp')
- input_grad: bfloat16 [24, 1024, 1024], P('dp')
- prefix_key_grad: float32 [96, 1024], P('prefix')
- prefix_value_grad: float32 [96, 1024], P('prefix')
Inputs may be any that keep to these rules, and one draw needn't show every extreme that they name: `segment_ids`: within a row segment numbers never fall; each segment holds 1 to 512 positions, and some segment of each row exactly that many.
All inputs are finite; a program needn't handle non-finite values. No bound on the sum of `key_mask` on one device may be relied on, other than what follows from the above.
Results may differ from a plain program's by a relative error of at most 0.015.
Values may be sent and summed in bfloat16 or wider, within the bound.
A program may use at most 256 MiB of HBM per device.

v0:
```python
import jax
import jax.numpy as jnp
from jax import lax
from jax.sharding import PartitionSpec as P

HEADS = 16
HEAD_DIM = 64
ROW_LEN = 1024
PREFIX = 96


EPSILON = 1e-05
NEGATIVE = -1e30


def matmul(left, right):
    return jnp.dot(left, right, preferred_element_type=jnp.float32)


def matmul_back(left, right):
    return lax.dot_general(
        left, right, (((1,), (1,)), ((), ())), preferred_element_type=jnp.float32
    )


def layer_norm(values, gain, shift):
    center = values - jnp.mean(values, axis=-1, keepdims=True)
    spread = jnp.mean(center * center, axis=-1, keepdims=True)
    return center * lax.rsqrt(spread + EPSILON) * gain + shift


def gelu_exact(values):
    return jax.nn.gelu(values, approximate=False)


def visible(seg_row, pad_row):
    same_doc = (seg_row[:, None] == seg_row[None, :]) & (pad_row[None, :] == 1)
    return jnp.concatenate([same_doc, jnp.ones((ROW_LEN, PREFIX), jnp.bool_)], axis=1)


def masked_scores(heads_query, all_keys, allowed):
    plain_scores = jnp.einsum(
        "qhd,khd->hqk", heads_query, all_keys, preferred_element_type=jnp.float32
    ) * HEAD_DIM ** (-0.5)
    return jnp.where(allowed[None], plain_scores, NEGATIVE)


def body(
    hidden_in,
    cotangent,
    segment_ids,
    key_mask,
    prefix_keys,
    prefix_values,
    w_query,
    b_query,
    w_key,
    b_key,
    w_value,
    b_value,
    w_attn_out,
    b_attn_out,
    gain_attn,
    shift_attn,
    w_ffn_in,
    b_ffn_in,
    w_ffn_out,
    b_ffn_out,
    gain_ffn,
    shift_ffn,
):
    micro = hidden_in.shape[0]
    width = hidden_in.shape[2]
    group_size = lax.axis_size("prefix")
    share_rows = ROW_LEN // group_size
    offset = lax.axis_index("prefix") * share_rows
    heads_here = HEADS // group_size
    local_cols = width // group_size
    score_scale = HEAD_DIM ** (-0.5)
    shards = (w_query, w_key, w_value, w_attn_out, w_ffn_in, w_ffn_out)
    key_cols, value_cols = (
        lax.all_to_all(prefix_keys, "prefix", split_axis=1, concat_axis=0, tiled=True),
        lax.all_to_all(prefix_values, "prefix", split_axis=1, concat_axis=0, tiled=True),
    )
    key_grad_sum = jnp.zeros((PREFIX, local_cols), jnp.float32)
    value_grad_sum = jnp.zeros((PREFIX, local_cols), jnp.float32)
    outputs = []
    input_grads = []
    for batch_index in range(micro):
        row_in = hidden_in[batch_index]
        seg_row = segment_ids[batch_index]
        pad_row = key_mask[batch_index]
        own_rows = lax.dynamic_slice_in_dim(row_in, offset, share_rows, 0).astype(jnp.float32)
        cot_rows = lax.dynamic_slice_in_dim(cotangent[batch_index], offset, share_rows, 0).astype(
            jnp.float32
        )
        forward_set = (
            lax.all_gather(shards[0], "dp", axis=0, tiled=True),
            lax.all_gather(shards[1], "dp", axis=0, tiled=True),
            lax.all_gather(shards[2], "dp", axis=0, tiled=True),
            lax.all_gather(shards[3], "dp", axis=1, tiled=True),
            lax.all_gather(shards[4], "dp", axis=0, tiled=True),
            lax.all_gather(shards[5], "dp", axis=1, tiled=True),
        )
        query_full, key_full, value_full, proj_full, inner_full, outer_full = forward_set
        queries = (matmul(row_in, query_full) + b_query).astype(jnp.bfloat16)
        key_rows = (matmul(row_in, key_full) + b_key).astype(jnp.bfloat16)
        value_rows = (matmul(row_in, value_full) + b_value).astype(jnp.bfloat16)
        all_keys = jnp.concatenate([key_rows, key_cols], axis=0).reshape(
            ROW_LEN + PREFIX, heads_here, HEAD_DIM
        )
        all_values = jnp.concatenate([value_rows, value_cols], axis=0).reshape(
            ROW_LEN + PREFIX, heads_here, HEAD_DIM
        )
        heads_query = queries.reshape(ROW_LEN, heads_here, HEAD_DIM)
        allowed = visible(seg_row, pad_row)
        scores = masked_scores(heads_query, all_keys, allowed)
        top_score = jnp.max(scores, axis=-1, keepdims=True)
        log_total = top_score + jnp.log(
            jnp.sum(jnp.exp(scores - top_score), axis=-1, keepdims=True)
        )
        weights_low = jnp.exp(scores - log_total).astype(jnp.bfloat16)
        context = jnp.einsum(
            "hqk,khd->qhd", weights_low, all_values, preferred_element_type=jnp.float32
        )
        context = context.reshape(ROW_LEN, local_cols).astype(jnp.bfloat16)
        attended = (
            lax.psum_scatter(matmul(context, proj_full), "prefix", scatter_dimension=0, tiled=True)
            + b_attn_out
        )
        first_sum = own_rows + attended
        normed = layer_norm(first_sum, gain_attn, shift_attn)
        hidden_pre = (
            matmul(
                lax.all_gather(normed.astype(jnp.bfloat16), "prefix", axis=0, tiled=True),
                inner_full,
            )
            + b_ffn_in
        )
        activated = gelu_exact(hidden_pre).astype(jnp.bfloat16)
        branch = (
            lax.psum_scatter(
                matmul(activated, outer_full), "prefix", scatter_dimension=0, tiled=True
            )
            + b_ffn_out
        )
        second_sum = normed + branch
        backward_set = (
            lax.all_gather(shards[0], "dp", axis=0, tiled=True),
            lax.all_gather(shards[1], "dp", axis=0, tiled=True),
            lax.all_gather(shards[2], "dp", axis=0, tiled=True),
            lax.all_gather(shards[3], "dp", axis=1, tiled=True),
            lax.all_gather(shards[4], "dp", axis=0, tiled=True),
            lax.all_gather(shards[5], "dp", axis=1, tiled=True),
        )
        query_full, key_full, value_full, proj_full, inner_full, outer_full = backward_set
        result_rows, second_pull = jax.vjp(
            lambda values: layer_norm(values, gain_ffn, shift_ffn), second_sum
        )
        grad_second = second_pull(cot_rows)[0]
        output_full, grad_branch = (
            lax.all_gather(result_rows.astype(jnp.bfloat16), "prefix", axis=0, tiled=True),
            lax.all_gather(grad_second.astype(jnp.bfloat16), "prefix", axis=0, tiled=True),
        )
        grad_act = matmul_back(grad_branch, outer_full)
        gelu_pull = jax.vjp(gelu_exact, hidden_pre)[1]
        grad_pre = gelu_pull(grad_act)[0].astype(jnp.bfloat16)
        grad_normed = grad_second + lax.psum_scatter(
            matmul_back(grad_pre, inner_full), "prefix", scatter_dimension=0, tiled=True
        )
        first_pull = jax.vjp(lambda values: layer_norm(values, gain_attn, shift_attn), first_sum)[1]
        grad_first = first_pull(grad_normed)[0]
        grad_context = matmul_back(
            lax.all_gather(grad_first.astype(jnp.bfloat16), "prefix", axis=0, tiled=True), proj_full
        ).astype(jnp.bfloat16)
        scores = masked_scores(heads_query, all_keys, allowed)
        weights_soft = jnp.exp(scores - log_total)
        weights_low = weights_soft.astype(jnp.bfloat16)
        grad_heads = grad_context.reshape(ROW_LEN, heads_here, HEAD_DIM)
        grad_soft = jnp.einsum(
            "qhd,khd->hqk", grad_heads, all_values, preferred_element_type=jnp.float32
        )
        row_delta = jnp.sum(weights_soft * grad_soft, axis=-1, keepdims=True)
        grad_scores = (weights_soft * (grad_soft - row_delta)).astype(jnp.bfloat16)
        grad_query = jnp.einsum(
            "hqk,khd->qhd", grad_scores, all_keys, preferred_element_type=jnp.float32
        )
        grad_query = (grad_query * score_scale).reshape(ROW_LEN, local_cols).astype(jnp.bfloat16)
        grad_keys = jnp.einsum(
            "hqk,qhd->khd", grad_scores, heads_query, preferred_element_type=jnp.float32
        )
        grad_keys = (grad_keys * score_scale).reshape(ROW_LEN + PREFIX, local_cols)
        grad_values = jnp.einsum(
            "hqk,qhd->khd", weights_low, grad_heads, preferred_element_type=jnp.float32
        )
        grad_values = grad_values.reshape(ROW_LEN + PREFIX, local_cols)
        key_part = grad_keys[:ROW_LEN].astype(jnp.bfloat16)
        value_part = grad_values[:ROW_LEN].astype(jnp.bfloat16)
        key_grad_sum = key_grad_sum + grad_keys[ROW_LEN:]
        value_grad_sum = value_grad_sum + grad_values[ROW_LEN:]
        input_rows = grad_first + lax.psum_scatter(
            (
                matmul_back(grad_query, query_full)
                + matmul_back(key_part, key_full)
                + matmul_back(value_part, value_full)
            ).astype(jnp.bfloat16),
            "prefix",
            scatter_dimension=0,
            tiled=True,
        ).astype(jnp.float32)
        input_grads.append(
            lax.all_gather(input_rows.astype(jnp.bfloat16), "prefix", axis=0, tiled=True)
        )
        outputs.append(output_full)
    key_back, value_back = (
        lax.all_to_all(
            key_grad_sum.astype(jnp.bfloat16), "prefix", split_axis=0, concat_axis=1, tiled=True
        ).astype(key_grad_sum.dtype),
        lax.all_to_all(
            value_grad_sum.astype(jnp.bfloat16), "prefix", split_axis=0, concat_axis=1, tiled=True
        ).astype(value_grad_sum.dtype),
    )
    key_total, value_total = lax.psum((key_back, value_back), "dp")
    return (jnp.stack(outputs), jnp.stack(input_grads), key_total, value_total)


def solution(mesh):
    return jax.shard_map(
        body,
        mesh=mesh,
        in_specs=(
            P("dp", None, None),
            P("dp", None, None),
            P("dp", None),
            P("dp", None),
            P("prefix", None),
            P("prefix", None),
            P("dp", "prefix"),
            P("prefix"),
            P("dp", "prefix"),
            P("prefix"),
            P("dp", "prefix"),
            P("prefix"),
            P("prefix", "dp"),
            P(),
            P(),
            P(),
            P("dp", "prefix"),
            P("prefix"),
            P("prefix", "dp"),
            P(),
            P(),
            P(),
        ),
        out_specs=(P("dp", None, None), P("dp", None, None), P("prefix", None), P("prefix", None)),
        check_vma=False,
    )
```

profile of v0, /device:TPU:0, one launch (start us, length us, event | category | flops | bytes accessed | tf_op | source)
XLA Modules:
  0.0 1692.5 jit_solution(9251448244042801248)
XLA Ops:
  9.4 6.3 all-to-all-start.1
  17.5 10.2 all_gather.43
  27.6 9.5 all_gather.44
  37.2 9.2 all_gather.42
  57.3 9.6 all_gather.45
  66.9 5.1 all-to-all-start
  72.4 11.2 fusion.204
  83.6 8.6 exponential_reduce_fusion
  92.6 9.3 fusion.102
  113.4 8.3 fusion.203
  121.6 8.7 exponential_reduce_fusion.1
  130.4 9.2 fusion.99
  151.8 8.1 fusion.205
  159.9 8.7 exponential_reduce_fusion.2
  168.7 9.2 fusion.96
  181.5 5.6 fusion.201
  187.2 75.2 %reduce-scatter.17.cloned.1.call-done = f32[256,1024]{1,0:T(8,128)} async-done(((f32[1024,1024]{1,0:T(8,128)}), f32[256,1024]{1,0:T(8,128)}) %reduce-scatter.17.cloned.1.call-update) | async-done | bytes 1048592 | tf_op jit(solution)/shard_map/reduce_scatter | solution.py:128
  262.4 79.6 %reduce-scatter.13.cloned.1.call-done = f32[256,1024]{1,0:T(8,128)} async-done(((f32[1024,1024]{1,0:T(8,128)}), f32[256,1024]{1,0:T(8,128)}) %reduce-scatter.13.cloned.1.call-update) | async-done | bytes 1048592 | tf_op jit(solution)/shard_map/reduce_scatter | solution.py:128
  350.0 44.0 %all-gather.18.cloned.1.call-done = bf16[1024,1024]{1,0:T(8,128)(2,1)} async-done(((bf16[256,1024]{1,0:T(8,128)(2,1)}), bf16[1024,1024]{1,0:T(8,128)(2,1)}) %all-gather.18.cloned.1.call-update) | async-done | bytes 2097168 | tf_op jit(solution)/shard_map/all_gather | solution.py:135
  394.1 6.6 fusion.213
  400.6 39.9 %all-gather.30.cloned.1.call-done = bf16[1024,1024]{1,0:T(8,128)(2,1)} async-done(((bf16[256,1024]{1,0:T(8,128)(2,1)}), bf16[1024,1024]{1,0:T(8,128)(2,1)}) %all-gather.30.cloned.1.call-update) | async-done | bytes 2097168 | tf_op jit(solution)/shard_map/all_gather | solution.py:135
  440.6 6.6 fusion.216
  447.1 39.5 %all-gather.26.cloned.1.call-done = bf16[1024,1024]{1,0:T(8,128)(2,1)} async-done(((bf16[256,1024]{1,0:T(8,128)(2,1)}), bf16[1024,1024]{1,0:T(8,128)(2,1)}) %all-gather.26.cloned.1.call-update) | async-done | bytes 2097168 | tf_op jit(solution)/shard_map/all_gather | solution.py:135
  486.6 33.9 %fusion.7 = (f32[1024,1024]{1,0:T(8,128)}, f32[1024,1024]{1,0:T(8,128)}, f32[1024,1024]{1,0:T(8,128)}, f32[1024,1024]{1,0:T(8,128)}) fusion(f32[1024]{0:T(1024)S(1)} %copy-done.72, f32[1024,1024]{1,0:T(8,128)} %fusion.216, f32[1024,1024]{1,0:T(8,128)} %fusion.213, bf16[1024,1024]{1,0:T(8,128)(2,1)} %all-gather.26.cloned.1.call-done, ...), kind=kOutput, calls=%fused_computation.27 | convolution fusion | flops 2345664512 | bytes 29364224 | tf_op jit(solution)/shard_map/dot_general | solution.py:17
  520.6 8.4 fusion.36
  529.5 8.6 fusion.38
  538.1 8.4 fusion.37
  546.6 5.7 fusion.200
  552.3 52.4 %reduce-scatter.15.cloned.1.call-done = f32[256,1024]{1,0:T(8,128)} async-done(((f32[1024,1024]{1,0:T(8,128)}), f32[256,1024]{1,0:T(8,128)}) %reduce-scatter.15.cloned.1.call-update) | async-done | bytes 1048592 | tf_op jit(solution)/shard_map/reduce_scatter | solution.py:142
  604.7 79.4 %reduce-scatter.23.cloned.1.call-done = f32[256,1024]{1,0:T(8,128)} async-done(((f32[1024,1024]{1,0:T(8,128)}), f32[256,1024]{1,0:T(8,128)}) %reduce-scatter.23.cloned.1.call-update) | async-done | bytes 1048592 | tf_op jit(solution)/shard_map/reduce_scatter | solution.py:142
  684.1 79.5 %reduce-scatter.19.cloned.1.call-done = f32[256,1024]{1,0:T(8,128)} async-done(((f32[1024,1024]{1,0:T(8,128)}), f32[256,1024]{1,0:T(8,128)}) %reduce-scatter.19.cloned.1.call-update) | async-done | bytes 1048592 | tf_op jit(solution)/shard_map/reduce_scatter | solution.py:142
  777.7 41.9 %all-gather.40.cloned.1.call-done = bf16[1024,1024]{1,0:T(8,128)(2,1)} async-done(((bf16[256,1024]{1,0:T(8,128)(2,1)}), bf16[1024,1024]{1,0:T(8,128)(2,1)}) %all-gather.40.cloned.1.call-update) | async-done | bytes 2097168 | tf_op jit(solution)/shard_map/all_gather | solution.py:163
  819.7 12.0 fusion.64
  831.9 33.9 %all-gather.46.cloned.1.call-done = bf16[1024,1024]{1,0:T(8,128)(2,1)} async-done(((bf16[256,1024]{1,0:T(8,128)(2,1)}), bf16[1024,1024]{1,0:T(8,128)(2,1)}) %all-gather.46.cloned.1.call-update) | async-done | bytes 2097168 | tf_op jit(solution)/shard_map/all_gather | solution.py:163
  865.8 12.0 fusion.65
  877.8 34.1 %all-gather.34.cloned.1.call-done = bf16[1024,1024]{1,0:T(8,128)(2,1)} async-done(((bf16[256,1024]{1,0:T(8,128)(2,1)}), bf16[1024,1024]{1,0:T(8,128)(2,1)}) %all-gather.34.cloned.1.call-update) | async-done | bytes 2097168 | tf_op jit(solution)/shard_map/all_gather | solution.py:163
  911.9 12.0 fusion.63
  924.0 65.7 %reduce-scatter.29.cloned.1.call-done = f32[256,1024]{1,0:T(8,128)} async-done(((f32[1024,1024]{1,0:T(8,128)}), f32[256,1024]{1,0:T(8,128)}) %reduce-scatter.29.cloned.1.call-update) | async-done | bytes 1048592 | tf_op jit(solution)/shard_map/reduce_scatter | solution.py:168
  989.7 79.7 %reduce-scatter.33.cloned.1.call-done = f32[256,1024]{1,0:T(8,128)} async-done(((f32[1024,1024]{1,0:T(8,128)}), f32[256,1024]{1,0:T(8,128)}) %reduce-scatter.33.cloned.1.call-update) | async-done | bytes 1048592 | tf_op jit(solution)/shard_map/reduce_scatter | solution.py:168
  1069.4 80.2 %reduce-scatter.25.cloned.1.call-done = f32[256,1024]{1,0:T(8,128)} async-done(((f32[1024,1024]{1,0:T(8,128)}), f32[256,1024]{1,0:T(8,128)}) %reduce-scatter.25.cloned.1.call-update) | async-done | bytes 1048592 | tf_op jit(solution)/shard_map/reduce_scatter | solution.py:168
  1149.6 3.8 multiply_reduce_fusion.5
  1162.5 41.1 %all-gather.36.cloned.1.call-done = bf16[1024,1024]{1,0:T(8,128)(2,1)} async-done(((bf16[256,1024]{1,0:T(8,128)(2,1)}), bf16[1024,1024]{1,0:T(8,128)(2,1)}) %all-gather.36.cloned.1.call-update) | async-done | bytes 2097168 | tf_op jit(solution)/shard_map/all_gather | solution.py:174
  1206.0 10.5 convolution_bitcast_fusion.2
  1216.5 12.1 multiply_reduce_fusion.2
  1228.6 13.1 multiply_convert_fusion.2
  1241.8 3.8 fusion.24
  1252.6 12.4 multiply_reduce_fusion.1
  1271.4 17.0 %multiply_convert_fusion.1 = bf16[4,1024,1120]{1,2,0:T(8,128)(2,1)} fusion(f32[4,1024,1120]{1,2,0:T(8,128)} %get-tuple-element.96, f32[4,1024,1120]{1,2,0:T(8,128)} %get-tuple-element.87, f32[4,1024]{1,0:T(4,128)S(1)} %get-tuple-element.95, f32[4,1024]{1,0:T(4,128)S(1)} %copy-done.42), kind=kLoop, calls=%fused_computation.8 | loop fusion | flops 18350080 | bytes 45907968 | tf_op jit(solution)/shard_map/convert_element_type | solution.py:184
  1288.6 9.3 convolution_bitcast_fusion.1
  1307.7 5.4 fusion.94
  1316.3 12.0 multiply_reduce_fusion
  1328.3 13.3 multiply_convert_fusion
  1341.6 7.8 convolution_bitcast_fusion
  1362.5 35.7 %reduce-scatter.31.cloned.1.call-done = bf16[256,1024]{1,0:T(8,128)(2,1)} async-done(((bf16[1024,1024]{1,0:T(8,128)(2,1)}), bf16[256,1024]{1,0:T(8,128)(2,1)}) %reduce-scatter.31.cloned.1.call-update) | async-done | bytes 524304 | tf_op jit(solution)/shard_map/reduce_scatter | solution.py:201
  1400.3 65.3 %reduce-scatter.35.cloned.1.call-done = bf16[256,1024]{1,0:T(8,128)(2,1)} async-done(((bf16[1024,1024]{1,0:T(8,128)(2,1)}), bf16[256,1024]{1,0:T(8,128)(2,1)}) %reduce-scatter.35.cloned.1.call-update) | async-done | bytes 524304 | tf_op jit(solution)/shard_map/reduce_scatter | solution.py:201
  1467.7 19.8 %all-gather.28.cloned.1.call-done = bf16[1024,1024]{1,0:T(8,128)(2,1)} async-done(((bf16[256,1024]{1,0:T(8,128)(2,1)}), bf16[1024,1024]{1,0:T(8,128)(2,1)}) %all-gather.28.cloned.1.call-update) | async-done | bytes 2097168 | tf_op jit(solution)/shard_map/all_gather | solution.py:162
  1487.5 46.7 %all-gather.32.cloned.1.call-done = bf16[1024,1024]{1,0:T(8,128)(2,1)} async-done(((bf16[256,1024]{1,0:T(8,128)(2,1)}), bf16[1024,1024]{1,0:T(8,128)(2,1)}) %all-gather.32.cloned.1.call-update) | async-done | bytes 2097168 | tf_op jit(solution)/shard_map/all_gather | solution.py:162
  1534.2 6.5 pad_maximum_fusion
  1547.9 4.6 all-to-all-done.3
  1556.4 5.3 all-to-all-done.2
  1562.4 20.0 %all-gather.38.cloned.1.call-done = bf16[1024,1024]{1,0:T(8,128)(2,1)} async-done(((bf16[256,1024]{1,0:T(8,128)(2,1)}), bf16[1024,1024]{1,0:T(8,128)(2,1)}) %all-gather.38.cloned.1.call-update) | async-done | bytes 2097168 | tf_op jit(solution)/shard_map/all_gather | solution.py:212
  1582.5 46.2 %all-gather.44.cloned.1.call-done = bf16[1024,1024]{1,0:T(8,128)(2,1)} async-done(((bf16[256,1024]{1,0:T(8,128)(2,1)}), bf16[1024,1024]{1,0:T(8,128)(2,1)}) %all-gather.44.cloned.1.call-update) | async-done | bytes 2097168 | tf_op jit(solution)/shard_map/all_gather | solution.py:212
  1628.7 46.7 %all-gather.50.cloned.1.call-done = bf16[1024,1024]{1,0:T(8,128)(2,1)} async-done(((bf16[256,1024]{1,0:T(8,128)(2,1)}), bf16[1024,1024]{1,0:T(8,128)(2,1)}) %all-gather.50.cloned.1.call-update) | async-done | bytes 2097168 | tf_op jit(solution)/shard_map/all_gather | solution.py:212
  1675.4 6.5 pad_maximum_fusion.1
  (326 shorter events, 134.4 us)
Async XLA Ops:
  8.0 43.0 %copy-start.73 = (f32[256]{0:T(256)S(1)}, f32[256]{0:T(256)}, u32[]{:S(2)}) copy-start(f32[256]{0:T(256)} %param.29) | copy-start | bytes 3076
  9.4 57.5 %all-to-all-start.1 = ((bf16[24,4,256]{2,0,1:T(8,128)(2,1)}), bf16[24,4,256]{2,0,1:T(8,128)(2,1)S(1)}, u32[]{:S(2)}, u32[]{:S(2)}) async-start(bf16[24,4,256]{2,0,1:T(8,128)(2,1)} %bitcast.232), calls=%async_computation.1 | async-start | bytes 98304 | tf_op jit(solution)/shard_map/all_to_all | solution.py:82
  27.6 116.7 %copy-start.10 = (bf16[1024,256]{1,0:T(8,128)(2,1)}, bf16[1024,256]{1,0:T(8,128)(2,1)S(1)}, u32[]{:S(2)}) copy-start(bf16[1024,256]{1,0:T(8,128)(2,1)S(1)} %all_gather.43) | copy-start | bytes 1572868
  37.2 109.5 %copy-start.12 = (bf16[1024,256]{1,0:T(8,128)(2,1)}, bf16[1024,256]{1,0:T(8,128)(2,1)S(1)}, u32[]{:S(2)}) copy-start(bf16[1024,256]{1,0:T(8,128)(2,1)S(1)} %all_gather.44) | copy-start | bytes 1572868
  46.3 102.9 %copy-start.8 = (bf16[1024,256]{1,0:T(8,128)(2,1)}, bf16[1024,256]{1,0:T(8,128)(2,1)S(1)}, u32[]{:S(2)}) copy-start(bf16[1024,256]{1,0:T(8,128)(2,1)S(1)} %all_gather.42) | copy-start | bytes 1572868
  66.9 111.0 %copy-start.14 = (bf16[256,1024]{1,0:T(8,128)(2,1)}, bf16[256,1024]{1,0:T(8,128)(2,1)S(1)}, u32[]{:S(2)}) copy-start(bf16[256,1024]{1,0:T(8,128)(2,1)S(1)} %all_gather.45) | copy-start | bytes 1572868
  66.9 25.4 %all-to-all-start = ((bf16[24,4,256]{2,0,1:T(8,128)(2,1)}), bf16[24,4,256]{2,0,1:T(8,128)(2,1)S(1)}, u32[]{:S(2)}, u32[]{:S(2)}) async-start(bf16[24,4,256]{2,0,1:T(8,128)(2,1)} %bitcast.233), calls=%async_computation | async-start | bytes 98304 | tf_op jit(solution)/shard_map/all_to_all | solution.py:83
  72.0 115.1 %reduce-scatter.21.cloned.1.call-start = ((), (), s32[]{:S(2)}) async-start(), calls=%async_computation.26 | async-start | bytes 5242880 | tf_op jit(solution)/shard_map/reduce_scatter | solution.py:128
  72.4 79.4 %copy-start.37 = (bf16[96,4,64]{0,2,1:T(8,128)(2,1)}, bf16[96,4,64]{0,2,1:T(8,128)(2,1)S(1)}, u32[]{:S(2)}) copy-start(bf16[96,4,64]{0,2,1:T(8,128)(2,1)S(1)} %copy.43) | copy-start | bytes 147460
  92.3 9.6 copy-start.39
  92.5 76.1 %copy-start.24 = (bf16[96,4,64]{0,2,1:T(8,128)(2,1)}, bf16[96,4,64]{0,2,1:T(8,128)(2,1)S(1)}, u32[]{:S(2)}) copy-start(bf16[96,4,64]{0,2,1:T(8,128)(2,1)S(1)} %copy.41) | copy-start | bytes 147460
  104.7 157.7 %reduce-scatter.17.cloned.1.call-start = ((), (), s32[]{:S(2)}) async-start(), calls=%async_computation.22 | async-start | bytes 5242880 | tf_op jit(solution)/shard_map/reduce_scatter | solution.py:128
  110.3 11.4 copy-start.46
  113.4 17.0 %copy-start.33 = (bf16[1024,256]{0,1:T(8,128)(2,1)}, bf16[1024,256]{0,1:T(8,128)(2,1)S(1)}, u32[]{:S(2)}) copy-start(bf16[1024,256]{0,1:T(8,128)(2,1)S(1)} %fusion.120) | copy-start | bytes 1572868
  142.4 199.5 %reduce-scatter.13.cloned.1.call-start = ((), (), s32[]{:S(2)}) async-start(), calls=%async_computation.16 | async-start | bytes 5242880 | tf_op jit(solution)/shard_map/reduce_scatter | solution.py:128
  149.2 10.7 copy-start.48
  151.8 16.9 copy-start.35
  168.7 9.3 copy-start.43
  180.7 169.3 %all-gather.20.cloned.1.call-start = ((), (), s32[]{:S(2)}) async-start(), calls=%async_computation.18 | async-start | bytes 2359296 | tf_op jit(solution)/shard_map/all_gather | solution.py:102
  181.3 212.8 %all-gather.18.cloned.1.call-start = ((), (), s32[]{:S(2)}) async-start(), calls=%async_computation.17 | async-start | bytes 2621440 | tf_op jit(solution)/shard_map/all_gather | solution.py:135
  181.5 160.5 %copy-start.69 = (f32[1024]{0:T(1024)S(1)}, f32[1024]{0:T(1024)}, u32[]{:S(2)}) copy-start(f32[1024]{0:T(1024)} %param.35) | copy-start | bytes 12292
  345.3 55.3 %copy-start.63 = (f32[256]{0:T(256)}, f32[256]{0:T(256)S(1)}, u32[]{:S(2)}) copy-start(f32[256]{0:T(256)S(1)} %multiply_reduce_fusion.7) | copy-start | bytes 3076
  347.9 92.7 %all-gather.30.cloned.1.call-start = ((), (), s32[]{:S(2)}) async-start(), calls=%async_computation.27 | async-start | bytes 2621440 | tf_op jit(solution)/shard_map/all_gather | solution.py:135
  348.5 138.2 %all-gather.26.cloned.1.call-start = ((), (), s32[]{:S(2)}) async-start(), calls=%async_computation.23 | async-start | bytes 2621440 | tf_op jit(solution)/shard_map/all_gather | solution.py:135
  349.2 171.4 %all-gather.22.cloned.1.call-start = ((), (), s32[]{:S(2)}) async-start(), calls=%async_computation.19 | async-start | bytes 2359296 | tf_op jit(solution)/shard_map/all_gather | solution.py:103
  350.0 254.7 %reduce-scatter.15.cloned.1.call-start = ((), (), s32[]{:S(2)}) async-start(), calls=%async_computation.20 | async-start | bytes 5242880 | tf_op jit(solution)/shard_map/reduce_scatter | solution.py:142
  400.6 86.0 %copy-start.72 = (f32[1024]{0:T(1024)S(1)}, f32[1024]{0:T(1024)}, u32[]{:S(2)}) copy-start(f32[1024]{0:T(1024)} %param.39) | copy-start | bytes 12292
  529.0 155.1 %reduce-scatter.23.cloned.1.call-start = ((), (), s32[]{:S(2)}) async-start(), calls=%async_computation.28 | async-start | bytes 5242880 | tf_op jit(solution)/shard_map/reduce_scatter | solution.py:142
  538.1 225.5 %reduce-scatter.19.cloned.1.call-start = ((), (), s32[]{:S(2)}) async-start(), calls=%async_computation.24 | async-start | bytes 5242880 | tf_op jit(solution)/shard_map/reduce_scatter | solution.py:142
  546.5 217.0 %copy-start.70 = (f32[1024]{0:T(1024)S(1)}, f32[1024]{0:T(1024)}, u32[]{:S(2)}) copy-start(f32[1024]{0:T(1024)} %param.41) | copy-start | bytes 12292
  546.5 273.2 %all-gather.40.cloned.1.call-start = ((), (), s32[]{:S(2)}) async-start(), calls=%async_computation.35 | async-start | bytes 2621440 | tf_op jit(solution)/shard_map/all_gather | solution.py:163
  552.3 214.3 %copy-start.58 = (f32[1024]{0:T(1024)S(1)}, f32[1024]{0:T(1024)}, u32[]{:S(2)}) copy-start(f32[1024]{0:T(1024)} %param.42) | copy-start | bytes 12292
  773.1 92.6 %all-gather.46.cloned.1.call-start = ((), (), s32[]{:S(2)}) async-start(), calls=%async_computation.40 | async-start | bytes 2621440 | tf_op jit(solution)/shard_map/all_gather | solution.py:163
  775.4 136.5 %all-gather.34.cloned.1.call-start = ((), (), s32[]{:S(2)}) async-start(), calls=%async_computation.30 | async-start | bytes 2621440 | tf_op jit(solution)/shard_map/all_gather | solution.py:163
  777.7 212.0 %reduce-scatter.29.cloned.1.call-start = ((), (), s32[]{:S(2)}) async-start(), calls=%async_computation.36 | async-start | bytes 5242880 | tf_op jit(solution)/shard_map/reduce_scatter | solution.py:168
  831.7 237.7 %reduce-scatter.33.cloned.1.call-start = ((), (), s32[]{:S(2)}) async-start(), calls=%async_computation.41 | async-start | bytes 5242880 | tf_op jit(solution)/shard_map/reduce_scatter | solution.py:168
  877.8 271.8 %reduce-scatter.25.cloned.1.call-start = ((), (), s32[]{:S(2)}) async-start(), calls=%async_computation.31 | async-start | bytes 5242880 | tf_op jit(solution)/shard_map/reduce_scatter | solution.py:168
  923.9 229.4 %copy-start.68 = (f32[256]{0:T(256)S(1)}, f32[256]{0:T(256)}, u32[]{:S(2)}) copy-start(f32[256]{0:T(256)} %copy-done.67) | copy-start | bytes 3076
  923.9 229.5 %copy-start.66 = (f32[256]{0:T(256)S(1)}, f32[256]{0:T(256)}, u32[]{:S(2)}) copy-start(f32[256]{0:T(256)} %copy-done.65) | copy-start | bytes 3076
  923.9 279.6 %all-gather.36.cloned.1.call-start = ((), (), s32[]{:S(2)}) async-start(), calls=%async_computation.32 | async-start | bytes 2621440 | tf_op jit(solution)/shard_map/all_gather | solution.py:174
  1157.4 92.8 %all-gather.42.cloned.1.call-start = ((), (), s32[]{:S(2)}) async-start(), calls=%async_computation.37 | async-start | bytes 2621440 | tf_op jit(solution)/shard_map/all_gather | solution.py:174
  1159.6 144.0 %all-gather.48.cloned.1.call-start = ((), (), s32[]{:S(2)}) async-start(), calls=%async_computation.42 | async-start | bytes 2621440 | tf_op jit(solution)/shard_map/all_gather | solution.py:174
  1161.4 44.5 %copy-start.44 = (f32[4,1024]{1,0:T(4,128)S(1)}, f32[4,1024]{1,0:T(4,128)}, u32[]{:S(2)}) copy-start(f32[4,1024]{1,0:T(4,128)} %copy-done.43) | copy-start | bytes 49156
  1162.4 197.9 %reduce-scatter.27.cloned.1.call-start = ((), (), s32[]{:S(2)}) async-start(), calls=%async_computation.33 | async-start | bytes 2621440 | tf_op jit(solution)/shard_map/reduce_scatter | solution.py:201
  1206.0 10.5 copy-start.25
  1206.0 10.5 copy-start.36
  1228.6 13.2 copy-start.54
  1252.5 12.5 copy-start.23
  1252.6 15.2 copy-start.13
  1288.5 109.7 %reduce-scatter.31.cloned.1.call-start = ((), (), s32[]{:S(2)}) async-start(), calls=%async_computation.38 | async-start | bytes 2621440 | tf_op jit(solution)/shard_map/reduce_scatter | solution.py:201
  1288.5 10.4 copy-start
  1288.5 10.4 copy-start.52
  1328.3 137.3 %reduce-scatter.35.cloned.1.call-start = ((), (), s32[]{:S(2)}) async-start(), calls=%async_computation.43 | async-start | bytes 2621440 | tf_op jit(solution)/shard_map/reduce_scatter | solution.py:201
  1358.4 39.8 %copy-start.5 = (f32[256,1024]{1,0:T(8,128)S(1)}, f32[256,1024]{1,0:T(8,128)}, u32[]{:S(2)}) copy-start(f32[256,1024]{1,0:T(8,128)} %get-tuple-element.72) | copy-start | bytes 3145732
  1358.4 39.8 %copy-start.60 = (f32[256]{0:T(256)S(1)}, f32[256]{0:T(256)}, u32[]{:S(2)}) copy-start(f32[256]{0:T(256)} %copy-done.59) | copy-start | bytes 3076
  1358.4 109.3 %all-gather.24.cloned.1.call-start = ((), (), s32[]{:S(2)}) async-start(), calls=%async_computation.21 | async-start | bytes 2621440 | tf_op jit(solution)/shard_map/all_gather | solution.py:162
  1359.0 128.5 %all-gather.28.cloned.1.call-start = ((), (), s32[]{:S(2)}) async-start(), calls=%async_computation.25 | async-start | bytes 2621440 | tf_op jit(solution)/shard_map/all_gather | solution.py:162
  1359.7 174.5 %all-gather.32.cloned.1.call-start = ((), (), s32[]{:S(2)}) async-start(), calls=%async_computation.29 | async-start | bytes 2621440 | tf_op jit(solution)/shard_map/all_gather | solution.py:162
  1360.3 222.2 %all-gather.38.cloned.1.call-start = ((), (), s32[]{:S(2)}) async-start(), calls=%async_computation.34 | async-start | bytes 2621440 | tf_op jit(solution)/shard_map/all_gather | solution.py:212
  1362.4 266.3 %all-gather.44.cloned.1.call-start = ((), (), s32[]{:S(2)}) async-start(), calls=%async_computation.39 | async-start | bytes 2621440 | tf_op jit(solution)/shard_map/all_gather | solution.py:212
  1400.2 275.1 %all-gather.50.cloned.1.call-start = ((), (), s32[]{:S(2)}) async-start(), calls=%async_computation.44 | async-start | bytes 2621440 | tf_op jit(solution)/shard_map/all_gather | solution.py:212
  1542.6 9.8 all-to-all-start.3
  1552.4 9.3 all-to-all-start.2
  1555.7 126.1 %all-reduce.6.cloned.1.call-start = ((), (), s32[]{:S(2)}) async-start(), calls=%async_computation.45 | async-start | bytes 393216 | tf_op jit(solution)/shard_map/psum | solution.py:223
  (46 other events, 163.6 us)
Sparse Core Ops, SparseCore 0:
  104.8 77.2 reduce-scatter.20
  185.1 77.2 reduce-scatter.16
  264.7 77.2 reduce-scatter.12
  773.3 46.3 all-gather.39
  821.1 44.6 all-gather.45
  867.2 44.6 all-gather.33
  914.2 75.4 reduce-scatter.28
  992.1 77.2 reduce-scatter.32
  1072.3 77.2 reduce-scatter.24
  1360.6 71.0 all-gather.23
  1433.3 54.1 all-gather.27
  1489.0 45.1 all-gather.31
  1535.8 46.6 all-gather.37
  1584.0 44.6 all-gather.43
  1630.7 44.6 all-gather.49
Sparse Core Ops, SparseCore 1:
  183.2 27.7 all-gather.19
  348.0 46.0 all-gather.17
  396.2 44.3 all-gather.29
  442.2 44.3 all-gather.25
  488.7 26.8 all-gather.21
  529.1 75.5 reduce-scatter.14
  606.8 77.2 reduce-scatter.22
  686.3 77.1 reduce-scatter.18
  1157.5 46.0 all-gather.35
  1205.8 44.3 all-gather.41
  1252.3 44.3 all-gather.47
  1299.1 42.3 reduce-scatter.26
  1344.2 53.9 reduce-scatter.30
  1401.2 64.4 reduce-scatter.34
  1562.5 52.1 all-reduce.5
where the time goes:
time: 1700 us; the launch traced here: 1690 us
  waiting for transfers between devices  1160 us (68%)
  matrix products  296 us (17%)
  other arithmetic  123 us (7%)
  blocking collectives  38.5 us (2%)
  local copies, waits for them, and re-layouts  34 us (2%)
  starting transfers between devices  20.7 us (1%)
  between operations  17.3 us (1%)
    reduce_scatter x3, waiting for transfers between devices, body(): lax.psum_scatter(matmul_back(grad_pre, inner_full), 'prefix', scatter_dim...  226 us
    reduce_scatter x3, waiting for transfers between devices, body(): lax.psum_scatter(matmul(activated, outer_full), 'prefix', scatter_dimensi...  211 us
    reduce_scatter x3, waiting for transfers between devices, body(): lax.psum_scatter(matmul(context, proj_full), 'prefix', scatter_dimension=...  155 us
    all_gather x3, waiting for transfers between devices, body(): lax.all_gather(normed.astype(jnp.bfloat16), 'prefix', axis=0, tiled=True)  123 us
    all_gather x3, waiting for transfers between devices, body(): lax.all_gather(input_rows.astype(jnp.bfloat16), 'prefix', axis=0, tiled=T...  113 us
    all_gather x3, waiting for transfers between devices, body(): lax.all_gather(grad_second.astype(jnp.bfloat16), 'prefix', axis=0, tiled=...  110 us
    dot_general x18, matrix products, matmul(): return jnp.dot(left, right, preferred_element_type=jnp.float32)  102 us
    reduce_scatter x3, waiting for transfers between devices, body(): lax.psum_scatter((matmul_back(grad_query, query_full) + matmul_back(key_p...  101 us
  transfers between devices with their start and end apart: 34, of which 25 were waited for; matrix products, arithmetic and copies ran while one was open for 24% of the time, Pallas kernels for 0%

commit v1 on v0

v1 whole, which is shorter than its diff:
```python
import functools
import jax
import jax.numpy as jnp
from jax import lax
from jax.experimental import pallas as pl
from jax.experimental.pallas import tpu as pltpu
from jax.sharding import PartitionSpec as P

L = 1024
D = 1024
PRE = 96
BLK = 128
NEG = -1e30
CLASSES = (2, 3, 4, 5, 6, 8)
bf16 = jnp.bfloat16
f32 = jnp.float32


def nt(a, b):
    return lax.dot_general(a, b, (((1,), (1,)), ((), ())), preferred_element_type=f32)


def nn(a, b):
    return jnp.dot(a, b, preferred_element_type=f32)


def stack_heads(tile):
    lane = lax.broadcasted_iota(jnp.int32, tile.shape, 1)
    zero = jnp.zeros_like(tile)
    return jnp.concatenate([jnp.where(lane < 64, tile, zero), jnp.where(lane >= 64, tile, zero)], axis=0)


def windows(seg):
    tiles = seg.shape[-1] // BLK
    first = seg[..., ::BLK]
    last = seg[..., BLK - 1 :: BLK]
    start = jnp.sum((seg[..., None, :] < first[..., :, None]).astype(jnp.int32), axis=-1) // BLK
    stop = (jnp.sum((seg[..., None, :] <= last[..., :, None]).astype(jnp.int32), axis=-1) + BLK - 1) // BLK
    need = stop - start
    size = jnp.full_like(need, CLASSES[-1])
    for n in reversed(CLASSES[:-1]):
        size = jnp.where(need <= n, n, size)
    start = jnp.minimum(start, tiles - size)
    return jnp.stack([start, size], axis=-1)


def attn_fwd_kernel(rows, win, x, w, b, pk, pv, segk, segq, qkv, ctx, lse, kx, vt):
    row = pl.program_id(0)
    y = nn(x[0], w[0]) + b[0]
    q = (y[:, :256].astype(bf16) * 0.125).astype(bf16)
    qkv[0, 0, :, :256] = q
    kv = y[:, 256:].astype(bf16)
    qkv[0, 0, :, 256:] = kv
    kx[:L] = kv[:, :256]
    kx[L:] = pk[0]
    vt[:, :L] = kv[:, 256:].T
    vt[:, L:] = pv[0].T

    def tile(t, carry):
        start = win[row, t, 0]
        size = win[row, t, 1]
        q0 = pl.multiple_of(t * BLK, BLK)
        k0 = pl.multiple_of(start * BLK, BLK)

        def run(n):
            W = n * BLK
            mask = segk[0, pl.ds(k0, W), :] == segq[0, :, pl.ds(q0, BLK)]
            for p in range(2):
                lanes = slice(128 * p, 128 * p + 128)
                q2 = stack_heads(qkv[0, 0, pl.ds(q0, BLK), lanes])
                s = nt(kx[pl.ds(k0, W), lanes], q2)
                s = jnp.concatenate([jnp.where(mask, s[:, :128], NEG), jnp.where(mask, s[:, 128:], NEG)], axis=1)
                sp = nt(kx[L : L + PRE, lanes], q2)
                top = jnp.maximum(jnp.max(s, axis=0, keepdims=True), jnp.max(sp, axis=0, keepdims=True))
                e = jnp.exp(s - top)
                ep = jnp.exp(sp - top)
                total = jnp.sum(e, axis=0, keepdims=True) + jnp.sum(ep, axis=0, keepdims=True)
                o = nn(vt[lanes, pl.ds(k0, W)], e.astype(bf16)) + nn(vt[lanes, L : L + PRE], ep.astype(bf16))
                o = o * (1.0 / total)
                o = jnp.concatenate([o[:64, :128], o[64:, 128:]], axis=0)
                ctx[0, pl.ds(q0, BLK), lanes] = o.T.astype(bf16)
                lt = top + jnp.log(total)
                lse[0, 0, 2 * p : 2 * p + 1, pl.ds(q0, BLK)] = lt[:, :128]
                lse[0, 0, 2 * p + 1 : 2 * p + 2, pl.ds(q0, BLK)] = lt[:, 128:]

        for n in CLASSES:
            pl.when(size == n)(functools.partial(run, n))
        return carry

    lax.fori_loop(0, L // BLK, tile, 0)


def attn_fwd(rows, win, x, w, b, pk, pv, segk, segq):
    R = rows.shape[0]
    row = lambda r, g, *_: (r, 0, 0)
    grp = lambda r, g, *_: (g, 0, 0)
    return pl.pallas_call(
        attn_fwd_kernel,
        grid_spec=pltpu.PrefetchScalarGridSpec(
            num_scalar_prefetch=2,
            grid=(R, 4),
            in_specs=[
                pl.BlockSpec((1, L, D), lambda r, g, rows, win: (rows[r], 0, 0)),
                pl.BlockSpec((1, D, 768), grp),
                pl.BlockSpec((1, 1, 768), grp),
                pl.BlockSpec((1, 128, 256), grp),
                pl.BlockSpec((1, 128, 256), grp),
                pl.BlockSpec((1, L, 128), row),
                pl.BlockSpec((1, 1, L), row),
            ],
            out_specs=[
                pl.BlockSpec((1, 1, L, 768), lambda r, g, *_: (r, g, 0, 0)),
                pl.BlockSpec((1, L, 256), lambda r, g, *_: (r, 0, g)),
                pl.BlockSpec((1, 1, 4, L), lambda r, g, *_: (r, g, 0, 0)),
            ],
            scratch_shapes=[pltpu.VMEM((L + 128, 256), bf16), pltpu.VMEM((256, L + 128), bf16)],
        ),
        out_shape=[
            jax.ShapeDtypeStruct((R, 4, L, 768), bf16),
            jax.ShapeDtypeStruct((R, L, D), bf16),
            jax.ShapeDtypeStruct((R, 4, 4, L), f32),
        ],
        compiler_params=pltpu.CompilerParams(vmem_limit_bytes=48 << 20),
        name="attn_fwd",
    )(rows, win, x, w, b, pk, pv, segk, segq)


def attn_bwd_kernel(r, rows, win, qkv, ctx, gctx, lse, pk, pv, segk, segq, gfirst, w, *rest):
    gin, pkg, pvg, dqt, dall, delta = rest[-6:]
    row = r
    g = pl.program_id(0)
    prod = gctx[0].astype(f32) * ctx[0].astype(f32)
    head = lax.broadcasted_iota(jnp.int32, (8, 256), 0)
    lane = lax.broadcasted_iota(jnp.int32, (8, 256), 1)
    pick = (lane // 64 == head).astype(f32)
    delta[...] = lax.dot_general(
        pick, prod, (((1,), (1,)), ((), ())), precision=lax.Precision.HIGHEST, preferred_element_type=f32
    )

    def block(kt, vt, mask, p, q0, W, first):
        n = kt.shape[0]
        lanes = slice(128 * p, 128 * p + 128)
        k2 = stack_heads(kt)
        v2 = stack_heads(vt)
        qw = qkv[0, 0, pl.ds(q0, W), lanes]
        dow = gctx[0, pl.ds(q0, W), lanes]
        s = nt(k2, qw)
        dp = nt(v2, dow)
        ps, ds = [], []
        for h in range(2):
            lrow = lse[0, 0, 2 * p + h : 2 * p + h + 1, pl.ds(q0, W)]
            drow = delta[2 * p + h : 2 * p + h + 1, pl.ds(q0, W)]
            sh = s[h * n : h * n + n] - lrow
            if mask is not None:
                sh = jnp.where(mask, sh, NEG)
            ph = jnp.exp(sh)
            ps.append(ph.astype(bf16))
            ds.append((ph * (dp[h * n : h * n + n] - drow)).astype(bf16))
        pb = jnp.concatenate(ps, axis=0)
        db = jnp.concatenate(ds, axis=0)
        dv = nn(pb, dow)
        dk = nn(db, qw)
        part = nn(k2.T, db)
        if first:
            dqt[lanes, pl.ds(q0, W)] = part
        else:
            dqt[lanes, pl.ds(q0, W)] += part
        lane = lax.broadcasted_iota(jnp.int32, (n, 128), 1)
        return jnp.where(lane < 64, dk[:n], dk[n:]), jnp.where(lane < 64, dv[:n], dv[n:])

    for p in range(2):
        lanes = slice(128 * p, 128 * p + 128)
        sk = jnp.zeros((PRE, 128), f32)
        sv = jnp.zeros((PRE, 128), f32)
        for c in range(2):
            dk, dv = block(pk[0, :PRE, lanes], pv[0, :PRE, lanes], None, p, c * 512, 512, True)
            sk = sk + dk
            sv = sv + dv
        pkg[:, lanes] = sk
        pvg[:, lanes] = sv

    def tile(t, carry):
        start = win[row, t, 0]
        size = win[row, t, 1]
        k0 = pl.multiple_of(t * BLK, BLK)
        q0 = pl.multiple_of(start * BLK, BLK)

        def run(n):
            W = n * BLK
            sk = segk[0, pl.ds(k0, BLK), :]
            sq = segq[0, :, pl.ds(q0, W)]
            mask = jnp.concatenate([sk] * n, axis=1) == sq
            for p in range(2):
                kt = qkv[0, 0, pl.ds(k0, BLK), 256 + 128 * p : 384 + 128 * p]
                vt = qkv[0, 0, pl.ds(k0, BLK), 512 + 128 * p : 640 + 128 * p]
                dk, dv = block(kt, vt, mask, p, q0, W, False)
                dall[g, pl.ds(k0, BLK), 256 + 128 * p : 384 + 128 * p] = dk.astype(bf16)
                dall[g, pl.ds(k0, BLK), 512 + 128 * p : 640 + 128 * p] = dv.astype(bf16)

        for n in CLASSES:
            pl.when(size == n)(functools.partial(run, n))
        return carry

    lax.fori_loop(0, L // BLK, tile, 0)
    dall[g, :, :256] = (dqt[...].T * 0.125).astype(bf16)

    @pl.when(g == 3)
    def _():
        def cols(c, carry):
            c0 = pl.multiple_of(c * 256, 256)
            acc = gfirst[0, :, pl.ds(c0, 256)].astype(f32)
            for i in range(4):
                acc = acc + nt(dall[i], w[i, pl.ds(c0, 256), :])
            gin[0, :, pl.ds(c0, 256)] = acc.astype(bf16)
            return carry

        lax.fori_loop(0, 4, cols, 0)


def attn_bwd(r, rows, win, qkv, ctx, gctx, lse, pk, pv, segk, segq, gfirst, w, into=None):
    row = lambda g, *_: (r, 0, 0)
    grp = lambda g, *_: (g, 0, 0)
    rg = lambda g, *_: (r, g, 0, 0)
    cg = lambda g, *_: (r, 0, g)
    extra = [] if into is None else [into]
    return pl.pallas_call(
        functools.partial(attn_bwd_kernel, r),
        grid_spec=pltpu.PrefetchScalarGridSpec(
            num_scalar_prefetch=2,
            grid=(4,),
            in_specs=[
                pl.BlockSpec((1, 1, L, 768), rg),
                pl.BlockSpec((1, L, 256), cg),
                pl.BlockSpec((1, L, 256), cg),
                pl.BlockSpec((1, 1, 4, L), rg),
                pl.BlockSpec((1, 128, 256), grp),
                pl.BlockSpec((1, 128, 256), grp),
                pl.BlockSpec((1, L, 128), row),
                pl.BlockSpec((1, 1, L), row),
                pl.BlockSpec((1, L, D), row),
                pl.BlockSpec((4, D, 768), lambda g, *_: (0, 0, 0)),
            ]
            + [pl.BlockSpec(memory_space=pl.ANY) for _ in extra],
            out_specs=[
                pl.BlockSpec((1, L, D), lambda g, rows, win: (rows[r], 0, 0)),
                pl.BlockSpec((PRE, 256), lambda g, *_: (0, g)),
                pl.BlockSpec((PRE, 256), lambda g, *_: (0, g)),
            ],
            scratch_shapes=[
                pltpu.VMEM((256, L), f32),
                pltpu.VMEM((4, L, 768), bf16),
                pltpu.VMEM((8, L), f32),
            ],
        ),
        out_shape=[
            jax.ShapeDtypeStruct((3, L, D), bf16),
            jax.ShapeDtypeStruct((PRE, D), f32),
            jax.ShapeDtypeStruct((PRE, D), f32),
        ],
        input_output_aliases={12: 0} if extra else {},
        compiler_params=pltpu.CompilerParams(vmem_limit_bytes=56 << 20),
        name="attn_bwd",
    )(rows, win, qkv, ctx, gctx, lse, pk, pv, segk, segq, gfirst, w, *extra)


HC = 512
TM = 512
EPS = 1e-5


ERF = (0.7978849414895208, 0.03633308441063725, -3.2594747109729314e-05, -5.5306315505082965e-05,
       3.964772884359942e-06, -1.3226625462816106e-07, 1.7562766828961903e-09)


def gelu_parts(v):
    u = v * v
    w = jnp.minimum(u, 31.36)
    p = ERF[6] * w + ERF[5]
    for c in ERF[4::-1]:
        p = p * w + c
    phi = 0.5 * jnp.tanh(v * p) + 0.5
    return v * phi, phi


def norm_stats(z):
    mean = jnp.mean(z, axis=1, keepdims=True)
    c = z - mean
    var = jnp.mean(c * c, axis=1, keepdims=True)
    r = lax.rsqrt(var + EPS)
    return c * r, r


RC = 512


def tokens_kernel(rows, ctx, x, cot, wo, win, wout, bo, g1, s1, bi, b2, g2, s2, out, gf, gc, xhat, zbuf, low, act, gp, rs, vb):
    M = TM

    def dot_cols(i, carry):
        c0 = pl.multiple_of(i * 256, 256)
        zbuf[:, pl.ds(c0, 256)] = nn(ctx[...], wo[:, pl.ds(c0, 256)]) + x[:, pl.ds(c0, 256)].astype(f32)
        return carry

    lax.fori_loop(0, 4, dot_cols, 0, unroll=4)

    def ln1(i, carry):
        r0 = pl.multiple_of(i * RC, RC)
        n, r = norm_stats(zbuf[pl.ds(r0, RC), :] + bo[...])
        xhat[pl.ds(r0, RC), :] = n
        rs[pl.ds(r0, RC), :] = jnp.broadcast_to(r, (RC, 128))
        y = n * g1[...] + s1[...]
        zbuf[pl.ds(r0, RC), :] = y
        low[pl.ds(r0, RC), :] = y.astype(bf16)
        return carry

    lax.fori_loop(0, M // RC, ln1, 0)

    def up(i, carry):
        z, c = i // 2, i % 2
        c0 = pl.multiple_of(c * HC, HC)
        h0 = pl.multiple_of(i * HC, HC)
        h = nn(low[...], win[z, :, pl.ds(c0, HC)]) + bi[:, pl.ds(h0, HC)]
        a, d = gelu_parts(h)
        act[:, pl.ds(h0, HC)] = a.astype(bf16)
        gp[:, pl.ds(h0, HC)] = d.astype(bf16)
        vb[:, pl.ds(h0, HC)] = h.astype(bf16)
        return carry

    lax.fori_loop(0, 8, up, 0, unroll=8)

    def down(i, carry):
        c0 = pl.multiple_of(i * 256, 256)
        zbuf[:, pl.ds(c0, 256)] += nn(act[...], wout[:, pl.ds(c0, 256)])
        return carry

    lax.fori_loop(0, 4, down, 0, unroll=4)

    def ln2(i, carry):
        r0 = pl.multiple_of(i * RC, RC)
        n, r = norm_stats(zbuf[pl.ds(r0, RC), :] + b2[...])
        out[pl.ds(r0, RC), :] = (n * g2[...] + s2[...]).astype(bf16)
        g = cot[pl.ds(r0, RC), :].astype(f32) * g2[...]
        m1 = jnp.mean(g, axis=1, keepdims=True)
        m2 = jnp.mean(g * n, axis=1, keepdims=True)
        d = (g - m1 - n * m2) * r
        zbuf[pl.ds(r0, RC), :] = d
        low[pl.ds(r0, RC), :] = d.astype(bf16)
        return carry

    lax.fori_loop(0, M // RC, ln2, 0)

    def back(i, carry):
        h0 = pl.multiple_of(i * HC, HC)
        d = nt(low[...], wout[pl.ds(h0, HC), :])
        v = vb[:, pl.ds(h0, HC)].astype(f32)
        slope = gp[:, pl.ds(h0, HC)].astype(f32) + v * (jnp.exp(-0.5 * v * v) * 0.3989422804014327)
        act[:, pl.ds(h0, HC)] = (d * slope).astype(bf16)
        return carry

    lax.fori_loop(0, 8, back, 0, unroll=8)

    def back2(i, carry):
        c0 = pl.multiple_of(i * 256, 256)
        acc = zbuf[:, pl.ds(c0, 256)]
        for z in range(4):
            acc = acc + nt(act[:, 1024 * z : 1024 * z + 1024], win[z, pl.ds(c0, 256), :])
        zbuf[:, pl.ds(c0, 256)] = acc
        return carry

    lax.fori_loop(0, 4, back2, 0, unroll=4)

    def ln1b(i, carry):
        r0 = pl.multiple_of(i * RC, RC)
        n = xhat[pl.ds(r0, RC), :]
        g = zbuf[pl.ds(r0, RC), :] * g1[...]
        m1 = jnp.mean(g, axis=1, keepdims=True)
        m2 = jnp.mean(g * n, axis=1, keepdims=True)
        d = (g - m1 - n * m2) * rs[pl.ds(r0, RC), 0:1]
        gf[pl.ds(r0, RC), :] = d.astype(bf16)
        return carry

    lax.fori_loop(0, M // RC, ln1b, 0)

    def gcols(i, carry):
        c0 = pl.multiple_of(i * 256, 256)
        gc[:, pl.ds(c0, 256)] = nt(gf[...], wo[pl.ds(c0, 256), :]).astype(bf16)
        return carry

    lax.fori_loop(0, 4, gcols, 0, unroll=4)


def tokens(rows, ctx, x, cot, wo, win, wout, bo, g1, s1, bi, b2, g2, s2):
    R = ctx.shape[0]
    per = L // TM
    own = pl.BlockSpec((None, TM, D), lambda i, rows: (i // per, i % per, 0))
    pick = pl.BlockSpec((None, TM, D), lambda i, rows: (rows[i // per], i % per, 0))
    whole = lambda a: pl.BlockSpec(a.shape, lambda i, rows: (0,) * a.ndim, pipeline_mode=pl.Buffered(1))
    consts = (wo, win, wout, bo, g1, s1, bi, b2, g2, s2)
    return pl.pallas_call(
        tokens_kernel,
        grid_spec=pltpu.PrefetchScalarGridSpec(
            num_scalar_prefetch=1,
            grid=(R * per,),
            in_specs=[own, pick, pick] + [whole(a) for a in consts],
            out_specs=[pick, own, own],
            scratch_shapes=[
                pltpu.VMEM((TM, D), f32),
                pltpu.VMEM((TM, D), f32),
                pltpu.VMEM((TM, D), bf16),
                pltpu.VMEM((TM, 4 * D), bf16),
                pltpu.VMEM((TM, 4 * D), bf16),
                pltpu.VMEM((TM, 128), f32),
                pltpu.VMEM((TM, 4 * D), bf16),
            ],
        ),
        out_shape=[
            jax.ShapeDtypeStruct((3, L, D), bf16),
            jax.ShapeDtypeStruct((R, L, D), bf16),
            jax.ShapeDtypeStruct((R, L, D), bf16),
        ],
        compiler_params=pltpu.CompilerParams(vmem_limit_bytes=60 << 20),
        name="tokens",
    )(rows, ctx, x, cot, *consts)


KINDS = 10
STEPS = ((0, 0), (1, -1), (1, 1), (2, -1), (2, 1), (3, -1), (3, 1))


def gather_kernel(pre_s, vec_s, wq, wk, wv, wo_s, wi_s, wu_s, pre, vec, qkv, wo, wi, wu, lsem, ssem, rsem):
    d = lax.axis_index("dp")
    z = lax.axis_index("prefix")
    core, xx, yy = d % 2, (d // 2) % 2, d // 4
    dc = d + 1 - 2 * core
    dx = d + 2 - 4 * xx
    dy = d + 4 - 8 * yy
    dxy = dx + dy - d

    def region(pay, zz, dd, half=None):
        if pay >= 4:
            return (pre, vec)[pay - 4].at[zz]
        if pay == 0:
            n, ref = 128, lambda o, s: qkv.at[zz, pl.ds(128 * dd + o, s), :]
        elif pay == 1:
            n, ref = 256, lambda o, s: wo.at[pl.ds(256 * zz + o, s), pl.ds(128 * dd, 128)]
        elif pay == 2:
            n, ref = 128, lambda o, s: wi.at[zz, pl.ds(128 * dd + o, s), :]
        else:
            n, ref = 1024, lambda o, s: wu.at[pl.ds(1024 * zz + o, s), pl.ds(128 * dd, 128)]
        return ref(0, n) if half is None else ref(half * (n // 2), n // 2)

    local = [
        pltpu.make_async_copy(src, dst, lsem.at[i])
        for i, (src, dst) in enumerate(
            [
                (wq, qkv.at[z, pl.ds(128 * d, 128), 0:256]),
                (wk, qkv.at[z, pl.ds(128 * d, 128), 256:512]),
                (wv, qkv.at[z, pl.ds(128 * d, 128), 512:768]),
                (wo_s, region(1, z, d)),
                (wi_s, region(2, z, d)),
                (wu_s, region(3, z, d)),
                (pre_s, pre.at[z]),
                (vec_s, vec.at[z]),
            ]
        )
    ]
    for c in local:
        c.start()
    bar = pltpu.get_barrier_semaphore()

    def hello(dev):
        pl.semaphore_signal(bar, inc=1, device_id=dev, device_id_type=pl.DeviceIdType.MESH)

    for dd in (dc, dx, dy):
        hello((dd, z))

    @pl.when(z > 0)
    def _():
        hello((d, z - 1))

    @pl.when(z < 3)
    def _():
        hello((d, z + 1))

    peers = jnp.where(z > 0, 1, 0) + jnp.where(z < 3, 1, 0)
    pl.semaphore_wait(bar, 3 + peers)
    for c in local:
        c.wait()

    def copy(kind, pay, zz, dd, half, dev, skind):
        r = region(pay, zz, dd, half)
        return pltpu.make_async_remote_copy(
            src_ref=r, dst_ref=r, send_sem=ssem.at[pay * 4 + zz, skind], recv_sem=rsem.at[pay * 4 + zz, kind],
            device_id=dev, device_id_type=pl.DeviceIdType.MESH,
        )

    def guard(step, fn):
        delta, side = step
        zz = z + delta * side
        if delta == 0:
            fn(zz)
        elif side < 0:
            pl.when(z >= delta)(lambda: fn(zz))
        else:
            pl.when(z + delta <= 3)(lambda: fn(zz))

    def stage1(pay, step):
        def run(zz):
            delta, side = step
            if delta:
                copy(0, pay, zz, d, None, (d, z), 0).wait_recv()
            if side <= 0:
                pl.when(z < 3)(lambda: copy(0, pay, zz, d, None, (d, z + 1), 10).start())
            if side >= 0:
                pl.when(z > 0)(lambda: copy(0, pay, zz, d, None, (d, z - 1), 0).start())
            if pay >= 4:
                return
            copy(1, pay, zz, d, None, (dx, z), 1).start()
            copy(2, pay, zz, d, None, (dy, z), 2).start()
            copy(5, pay, zz, d, None, (dc, z), 5).start()
        guard(step, run)

    def stage2(pay, step):
        def run(zz):
            copy(1, pay, zz, dx, None, (dx, z), 1).wait_recv()
            copy(3, pay, zz, dx, 0, (dy, z), 3).start()
            copy(6, pay, zz, dx, None, (dc, z), 6).start()
            copy(2, pay, zz, dy, None, (dy, z), 2).wait_recv()
            copy(4, pay, zz, dy, 1, (dx, z), 4).start()
            copy(7, pay, zz, dy, None, (dc, z), 7).start()
        guard(step, run)

    def stage3(pay, step):
        def run(zz):
            copy(3, pay, zz, dxy, 0, (dy, z), 3).wait_recv()
            copy(8, pay, zz, dxy, 0, (dc, z), 8).start()
            copy(4, pay, zz, dxy, 1, (dx, z), 4).wait_recv()
            copy(9, pay, zz, dxy, 1, (dc, z), 9).start()
        guard(step, run)

    def stage4(pay, step):
        o = dc - d
        def run(zz):
            copy(5, pay, zz, d + o, None, (dc, z), 5).wait_recv()
            copy(6, pay, zz, dx + o, None, (dc, z), 6).wait_recv()
            copy(7, pay, zz, dy + o, None, (dc, z), 7).wait_recv()
            copy(8, pay, zz, dxy + o, 0, (dc, z), 8).wait_recv()
            copy(9, pay, zz, dxy + o, 1, (dc, z), 9).wait_recv()
        guard(step, run)

    def drain(pay, step):
        def run(zz):
            delta, side = step
            if side <= 0:
                pl.when(z < 3)(lambda: copy(0, pay, zz, d, None, (d, z + 1), 10).wait_send())
            if side >= 0:
                pl.when(z > 0)(lambda: copy(0, pay, zz, d, None, (d, z - 1), 0).wait_send())
            if pay >= 4:
                return
            copy(1, pay, zz, d, None, (dx, z), 1).wait_send()
            copy(2, pay, zz, d, None, (dy, z), 2).wait_send()
            copy(3, pay, zz, dx, 0, (dy, z), 3).wait_send()
            copy(4, pay, zz, dy, 1, (dx, z), 4).wait_send()
            copy(5, pay, zz, d, None, (dc, z), 5).wait_send()
            copy(6, pay, zz, dx, None, (dc, z), 6).wait_send()
            copy(7, pay, zz, dy, None, (dc, z), 7).wait_send()
            copy(8, pay, zz, dxy, 0, (dc, z), 8).wait_send()
            copy(9, pay, zz, dxy, 1, (dc, z), 9).wait_send()
        guard(step, run)

    items = [(pay, step) for pay in range(4) for step in STEPS]
    small = [(pay, step) for pay in (4, 5) for step in STEPS]
    n = len(items)
    for i in range(n + 6):
        if i < n:
            stage1(*items[i])
        if i < len(small):
            stage1(*small[i])
        if 0 <= i - 3 < n:
            stage2(*items[i - 3])
        if 0 <= i - 6 < n:
            stage3(*items[i - 6])
    for it in items:
        stage4(*it)
    for it in items + small:
        drain(*it)


def gather(pre, vec, wq, wk, wv, wo, wi, wu):
    any_ = pl.BlockSpec(memory_space=pl.ANY)
    return pl.pallas_call(
        gather_kernel,
        in_specs=[any_] * 8,
        out_specs=[any_] * 6,
        out_shape=[
            jax.ShapeDtypeStruct((4,) + pre.shape, pre.dtype),
            jax.ShapeDtypeStruct((4,) + vec.shape, vec.dtype),
            jax.ShapeDtypeStruct((4, D, 768), bf16),
            jax.ShapeDtypeStruct((D, D), bf16),
            jax.ShapeDtypeStruct((4, D, D), bf16),
            jax.ShapeDtypeStruct((4 * D, D), bf16),
        ],
        scratch_shapes=[
            pltpu.SemaphoreType.DMA((8,)),
            pltpu.SemaphoreType.DMA((24, KINDS + 1)),
            pltpu.SemaphoreType.DMA((24, KINDS)),
        ],
        compiler_params=pltpu.CompilerParams(collective_id=0, has_side_effects=True),
        name="gather",
    )(pre, vec, wq, wk, wv, wo, wi, wu)


def gather_plain(pre, vec, wq, wk, wv, wo, wi, wu):
    over = lambda v, axis, at: lax.all_gather(v, axis, axis=at, tiled=True)
    qkv = jnp.concatenate([over(w, "dp", 0) for w in (wq, wk, wv)], axis=1)
    up = over(wi, "dp", 0)
    return (
        lax.all_gather(pre, "prefix"),
        lax.all_gather(vec, "prefix"),
        lax.all_gather(qkv, "prefix"),
        over(over(wo, "dp", 1), "prefix", 0),
        lax.all_gather(up, "prefix"),
        over(over(wu, "dp", 1), "prefix", 0),
    )


def body(
    hidden_in, cotangent, segment_ids, key_mask, prefix_keys, prefix_values,
    w_query, b_query, w_key, b_key, w_value, b_value, w_attn_out, b_attn_out, gain_attn, shift_attn,
    w_ffn_in, b_ffn_in, w_ffn_out, b_ffn_out, gain_ffn, shift_ffn,
):
    z = lax.axis_index("prefix")
    side = z % 2
    rows = jnp.stack([2 * side, jnp.ones_like(side)]).astype(jnp.int32)
    pre = jnp.concatenate([prefix_keys, prefix_values], axis=0)
    vec = jnp.concatenate([b_query, b_key, b_value, b_ffn_in, jnp.zeros((256,), f32)]).reshape(8, 256)
    whole = gather if lax.axis_size("dp") == 8 and lax.axis_size("prefix") == 4 else gather_plain
    pre, vec, w_qkv, w_out, w_up, w_down = whole(
        pre, vec, w_query, w_key, w_value, w_attn_out, w_ffn_in, w_ffn_out
    )
    by_group = lambda p: jnp.pad(p.reshape(PRE, 4, 256).transpose(1, 0, 2), ((0, 0), (0, 128 - PRE), (0, 0)))
    pk, pv = by_group(pre[:, :24]), by_group(pre[:, 24:])
    b_qkv = vec[:, :3].reshape(4, 1, 768)
    b_up = vec[:, 3:7].reshape(1, 4 * D)
    line = lambda v: v.reshape(1, -1)

    seg = jnp.stack([jnp.where(side == 0, segment_ids[0], segment_ids[2]), segment_ids[1]])
    mask = jnp.stack([jnp.where(side == 0, key_mask[0], key_mask[2]), key_mask[1]])
    win = windows(seg)
    segk = jnp.broadcast_to(jnp.where(mask == 1, seg, -1)[:, :, None], (2, L, 128))
    segq = seg[:, None, :]

    qkv, ctx, lse = attn_fwd(rows, win, hidden_in, w_qkv, b_qkv, pk, pv, segk, segq)
    out, gfirst, gctx = tokens(
        rows, ctx, hidden_in, cotangent, w_out, w_up, w_down, line(b_attn_out), line(gain_attn), line(shift_attn),
        b_up, line(b_ffn_out), line(gain_ffn), line(shift_ffn),
    )
    pairs = [(i, i + 1 - 2 * (i % 2)) for i in range(lax.axis_size("prefix"))]
    swap = lambda v: lax.ppermute(lax.dynamic_slice_in_dim(v, rows[0], 1, 0), "prefix", pairs)
    put = lambda v, r: lax.dynamic_update_slice_in_dim(v, r, 2 - rows[0], 0)
    out_other = swap(out)
    args = (rows, win, qkv, ctx, gctx, lse, pk, pv, segk, segq, gfirst, w_qkv)
    gin, ku, vu = attn_bwd(0, *args)
    gin_other = swap(gin)
    gin, ks, vs = attn_bwd(1, *args, into=gin)
    unique = (z < 2).astype(f32)
    shared = (z == 0).astype(f32)
    both = jnp.stack([ku * unique + ks * shared, vu * unique + vs * shared])
    both = lax.psum(lax.psum_scatter(both, "prefix", scatter_dimension=1, tiled=True), "dp")
    return put(out, out_other), put(gin, gin_other), both[0], both[1]


def solution(mesh):
    return jax.shard_map(
        body,
        mesh=mesh,
        in_specs=(
            P("dp", None, None), P("dp", None, None), P("dp", None), P("dp", None),
            P("prefix", None), P("prefix", None),
            P("dp", "prefix"), P("prefix"), P("dp", "prefix"), P("prefix"), P("dp", "prefix"), P("prefix"),
            P("prefix", "dp"), P(), P(), P(),
            P("dp", "prefix"), P("prefix"), P("prefix", "dp"), P(), P(), P(),
        ),
        out_specs=(P("dp", None, None), P("dp", None, None), P("prefix", None), P("prefix", None)),
        check_vma=False,
    )
```

time: 1700 us -> 607 us (0.36)
  waiting for transfers between devices: 1160 us -> 101 us
  Pallas kernels: 0 us -> 460 us
  matrix products: 296 us -> 0 us
  other arithmetic: 123 us -> 5.82 us
  blocking collectives: 38.5 us -> 0 us
    reduce_scatter x12 -> x1, waiting for transfers between devices: 693 us -> 45.2 us  [body(): lax.psum_scatter(both, 'prefix', scatter_dimension=1, tiled=True)]
    pallas_call x0 -> x5, Pallas kernels: none -> 460 us  [the longest x1 144 us: gather(): pl.pallas_call(gather_kernel, in_specs=[any_] * 8, out_specs=[any_] * 6,...]
    all_gather x17 -> x0, waiting for transfers between devices: 456 us -> none  [the longest x3 123 us: body(): lax.all_gather(normed.astype(jnp.bfloat16), 'prefix', axis=0, tiled=True)]
    dot_general x51 -> x0, matrix products: 296 us -> none  [the longest x18 102 us: matmul(): return jnp.dot(left, right, preferred_element_type=jnp.float32)]
    convert_element_type x15 -> x0, other arithmetic: 62.6 us -> none  [the longest x3 43.4 us: body(): grad_scores = (weights_soft * (grad_soft - row_delta)).astype(jnp.bfloat16)]
    psum x1, waiting for transfers between devices: 0.01 us -> 55.6 us  [body(): lax.psum(lax.psum_scatter(both, 'prefix', scatter_dimension=1, tiled=True...]
    reduce_sum x13 -> x1, other arithmetic: 43.8 us -> 0.22 us  [windows(): jnp.sum((seg[..., None, :] < first[..., :, None]).astype(jnp.int32), axis...]
    all_gather x4 -> x0, blocking collectives: 38.5 us -> none  [the longest x1 10.2 us: body(): lax.all_gather(shards[0], 'dp', axis=0, tiled=True)]
  transfers between devices with their start and end apart: 34 -> 4, of which waited for: 25 -> 2; matrix products, arithmetic and copies ran while one was open for 24% -> 2% of each run, Pallas kernels for 0% -> 9%
where the time goes in v1:
time: 607 us; the launch traced here: 613 us
  Pallas kernels  460 us (76%)
  waiting for transfers between devices  101 us (17%)
  local copies, waits for them, and re-layouts  22.7 us (4%)
  between operations  14.5 us (2%)
  starting transfers between devices  9.49 us (2%)
    pallas_call x1, Pallas kernels, gather(): pl.pallas_call(gather_kernel, in_specs=[any_] * 8, out_specs=[any_] * 6,...  144 us
    pallas_call x1, Pallas kernels, tokens(): pl.pallas_call(tokens_kernel, grid_spec=pltpu.PrefetchScalarGridSpec(num_...  122 us
    pallas_call x2, Pallas kernels, attn_bwd(): pl.pallas_call(functools.partial(attn_bwd_kernel, r), grid_spec=pltpu.Pre...  105 us
    pallas_call x1, Pallas kernels, attn_fwd(): pl.pallas_call(attn_fwd_kernel, grid_spec=pltpu.PrefetchScalarGridSpec(nu...  89.3 us
    psum x1, waiting for transfers between devices, body(): lax.psum(lax.psum_scatter(both, 'prefix', scatter_dimension=1, tiled=True...  55.6 us
    reduce_scatter x1, waiting for transfers between devices, body(): lax.psum_scatter(both, 'prefix', scatter_dimension=1, tiled=True)  45.2 us
  transfers between devices with their start and end apart: 4, of which 2 were waited for; matrix products, arithmetic and copies ran while one was open for 2% of the time, Pallas kernels for 9%

profile of v1, /device:TPU:0, one launch (start us, length us, event | category | flops | bytes accessed | tf_op | source)
XLA Modules:
  0.0 613.4 jit_solution(12445654137368325386)
XLA Ops:
  7.2 0.0 reduce-scatter.2.cloned.1.call-start
  7.2 0.9 broadcast_select_fusion
  8.1 0.1 slice.45
  8.2 0.1 slice.46
  8.3 0.0 copy-start.6
  8.4 0.7 constant_dynamic-update-slice_fusion.4
  9.0 0.7 constant_dynamic-update-slice_fusion.3
  9.7 0.7 constant_dynamic-update-slice_fusion.2
  10.4 0.7 constant_dynamic-update-slice_fusion.1
  11.1 0.6 reshape.224.vec_s
  11.7 1.5 pad_maximum_fusion.1.pre_s
  13.2 143.7 %gather.1 = (bf16[4,48,1024]{2,1,0:T(8,128)(2,1)}, f32[4,8,256]{2,1,0:T(8,128)}, bf16[4,1024,768]{2,1,0:T(8,128)(2,1)}, bf16[1024,1024]{1,0:T(8,128)(2,1)}, bf16...) custom-call(bf16[48,1024]{1,0:T(8,128)(2,1)} %pad_maximum_fusion.1.pre_s, f32[8,256]{1,0:T(8,128)} %reshape.224.vec_s, ...), custom_call_target="tpu_custom_call" | custom-call | tf_op jit(solution)/shard_map/gather/pallas_call | solution.py:591
  156.9 0.8 slice.47
  157.7 0.8 slice.53
  158.4 0.2 convert_reduce_fusion.1
  158.7 0.1 copy.58
  158.8 0.1 copy.54
  158.8 1.1 fusion.5
  159.9 0.1 reshape.226
  160.1 0.1 reshape.227
  160.3 0.0 copy-start.2
  160.3 0.0 copy-start.3
  160.3 0.7 reshape.231.bi
  161.1 0.1 pad_add_fusion.1.win
  161.1 0.0 copy-start.5
  161.1 0.1 pad_add_fusion.2.rows
  161.2 0.0 copy-start.7
  161.2 0.3 broadcast_in_dim.28.segk
  161.6 0.0 copy-start.1
  161.6 89.3 %attn_fwd.1 = (bf16[2,4,1024,768]{3,2,1,0:T(8,128)(2,1)}, bf16[2,1024,1024]{2,1,0:T(8,128)(2,1)S(1)}, f32[2,4,4,1024]{3,2,1,0:T(4,128)S(1)}) custom-call(s32[2]{0:T(128)S(1)} %pad_add_fusion.2.rows, s32[2,8,2]{2,1,0:T(8,128)S(1)} %pad_add_fusion.1.win, bf16[3,1024,1024]{2,1,0:T(8,128)(2,1)} %x.7, bf16[4,1024,768]{2,1,0:T(8,128)(2,1)} %get-tuple-element.22.w, ...), custom_call_target="tpu_custom_call" | custom-call | tf_op jit(solution)/shard_map/attn_fwd/pallas_call | solution.py:97
  250.9 0.0 copy-done.6
  250.9 0.0 copy-done.2
  250.9 0.0 copy-done.3
  250.9 0.0 copy-done.5
  250.9 0.0 copy-done.7
  250.9 0.0 copy-done.1
  250.9 0.0 copy-start
  250.9 2.0 copy-done
  252.9 0.0 copy-start.4
  252.9 0.6 copy-done.4
  253.5 122.4 %tokens.1 = (bf16[3,1024,1024]{2,1,0:T(8,128)(2,1)}, bf16[2,1024,1024]{2,1,0:T(8,128)(2,1)}, bf16[2,1024,1024]{2,1,0:T(8,128)(2,1)}) custom-call(s32[2]{0:T(128)} %copy-done.7, bf16[2,1024,1024]{2,1,0:T(8,128)(2,1)} %copy-done, bf16[3,1024,1024]{2,1,0:T(8,128)(2,1)} %x.7, bf16[3,1024,1024]{2,1,0:T(8,128)(2,1)} %cot.1, ...), custom_call_target="tpu_custom_call" | custom-call | tf_op jit(solution)/shard_map/tokens/pallas_call | solution.py:399
  375.9 49.6 %attn_bwd.2 = (bf16[3,1024,1024]{2,1,0:T(8,128)(2,1)}, f32[96,1024]{1,0:T(8,128)}, f32[96,1024]{1,0:T(8,128)}) custom-call(s32[2]{0:T(128)} %copy-done.7, s32[2,8,2]{2,1,0:T(8,128)} %copy-done.5, bf16[2,4,1024,768]{3,2,1,0:T(8,128)(2,1)} %get-tuple-element.30.qkv, bf16[2,1024,1024]{2,1,0:T(8,128)(2,1)} %copy-done, ...), custom_call_target="tpu_custom_call" | custom-call | tf_op jit(solution)/shard_map/attn_bwd/pallas_call | solution.py:226
  425.5 3.1 constant_dynamic-slice_fusion
  428.6 9.4 %collective-permute-start.1 = (bf16[1,1024,1024]{2,1,0:T(8,128)(2,1)}, bf16[1,1024,1024]{2,1,0:T(8,128)(2,1)S(1)}, u32[]{:S(2)}, u32[]{:S(2)}) collective-permute-start(bf16[1,1024,1024]{2,1,0:T(8,128)(2,1)} %constant_dynamic-slice_fusion), channel_id=1, source_target_pairs={{0,1},{1,0},{2,3},{3,2},{4,5},{5,4},{6,7},{7,6},{8,9},{9,8},{10,11... | collective-permute-start | bytes 6291464 | tf_op jit(solution)/shard_map/ppermute | solution.py:659
  438.0 3.1 constant_dynamic-slice_fusion.1
  441.1 0.0 copy-start.9
  441.1 0.0 copy-start.8
  441.1 0.0 collective-permute-start
  441.1 55.2 %attn_bwd.3 = (bf16[3,1024,1024]{2,1,0:T(8,128)(2,1)}, f32[96,1024]{1,0:T(8,128)}, f32[96,1024]{1,0:T(8,128)}) custom-call(s32[2]{0:T(128)} %copy-done.7, s32[2,8,2]{2,1,0:T(8,128)} %copy-done.5, bf16[2,4,1024,768]{3,2,1,0:T(8,128)(2,1)} %get-tuple-element.30.qkv, bf16[2,1024,1024]{2,1,0:T(8,128)(2,1)} %copy-done, ...), custom_call_target="tpu_custom_call", output_to_operand_aliasing={{0}: (12, {})} | custom-call | tf_op jit(solution)/shard_map/attn_bwd/pallas_call | solution.py:226
  496.3 0.0 copy-done.9
  496.3 1.0 add_bitcast_fusion.1
  497.4 0.0 copy-done.8
  497.4 1.0 add_bitcast_fusion
  498.4 1.0 pad_maximum_fusion
  499.4 0.0 reduce-scatter.2.cloned.1.call-update
  499.4 0.0 all-reduce.4.cloned.1.call-start
  499.4 45.2 %reduce-scatter.2.cloned.1.call-done = f32[2,24,1024]{2,1,0:T(8,128)} async-done(((f32[2,96,1024]{2,1,0:T(8,128)}), f32[2,24,1024]{2,1,0:T(8,128)}) %reduce-scatter.2.cloned.1.call-update) | async-done | bytes 196624 | tf_op jit(solution)/shard_map/reduce_scatter | solution.py:669
  544.6 0.0 all-reduce.4.cloned.1.call-update
  544.6 55.6 %all-reduce.4.cloned.1.call-done = f32[2,24,1024]{2,1,0:T(8,128)} async-done(((f32[2,24,1024]{2,1,0:T(8,128)}), f32[2,24,1024]{2,1,0:T(8,128)}) %all-reduce.4.cloned.1.call-update) | async-done | bytes 196624 | tf_op jit(solution)/shard_map/psum | solution.py:669
  600.2 1.6 slice_bitcast_fusion
  601.8 0.0 collective-permute-done
  601.8 3.1 constant_dynamic-update-slice_fusion.6
  604.9 0.0 collective-permute-done.1
  604.9 1.5 constant_dynamic-update-slice_fusion.5
  (11 shorter events, 0.2 us)
Async XLA Ops:
  7.2 537.4 %reduce-scatter.2.cloned.1.call-start = ((), (), s32[]{:S(2)}) async-start(), calls=%async_computation.1 | async-start | bytes 983040 | tf_op jit(solution)/shard_map/reduce_scatter | solution.py:669
  8.3 242.6 %copy-start.6 = (s32[2,1,1024]{2,1,0:T(1,128)}, s32[2,1,1024]{2,1,0:T(1,128)S(1)}, u32[]{:S(2)}) copy-start(s32[2,1,1024]{2,1,0:T(1,128)S(1)} %broadcast_in_dim.29.segq) | copy-start | bytes 24580
  160.3 90.6 %copy-start.2 = (bf16[4,128,256]{2,1,0:T(8,128)(2,1)}, bf16[4,128,256]{2,1,0:T(8,128)(2,1)S(1)}, u32[]{:S(2)}) copy-start(bf16[4,128,256]{2,1,0:T(8,128)(2,1)S(1)} %pad.7.pk) | copy-start | bytes 786436
  160.3 90.6 %copy-start.3 = (bf16[4,128,256]{2,1,0:T(8,128)(2,1)}, bf16[4,128,256]{2,1,0:T(8,128)(2,1)S(1)}, u32[]{:S(2)}) copy-start(bf16[4,128,256]{2,1,0:T(8,128)(2,1)S(1)} %pad.8.pv) | copy-start | bytes 786436
  161.1 89.8 %copy-start.5 = (s32[2,8,2]{2,1,0:T(8,128)}, s32[2,8,2]{2,1,0:T(8,128)S(1)}, u32[]{:S(2)}) copy-start(s32[2,8,2]{2,1,0:T(8,128)S(1)} %pad_add_fusion.1.win) | copy-start | bytes 388
  161.2 89.7 %copy-start.7 = (s32[2]{0:T(128)}, s32[2]{0:T(128)S(1)}, u32[]{:S(2)}) copy-start(s32[2]{0:T(128)S(1)} %pad_add_fusion.2.rows) | copy-start | bytes 28
  161.6 89.4 %copy-start.1 = (s32[2,1024,128]{2,1,0:T(8,128)}, s32[2,1024,128]{2,1,0:T(8,128)S(1)}, u32[]{:S(2)}) copy-start(s32[2,1024,128]{2,1,0:T(8,128)S(1)} %broadcast_in_dim.28.segk) | copy-start | bytes 3145732
  250.9 2.0 copy-start
  252.9 0.6 copy-start.4
  428.6 176.3 %collective-permute-start.1 = (bf16[1,1024,1024]{2,1,0:T(8,128)(2,1)}, bf16[1,1024,1024]{2,1,0:T(8,128)(2,1)S(1)}, u32[]{:S(2)}, u32[]{:S(2)}) collective-permute-start(bf16[1,1024,1024]{2,1,0:T(8,128)(2,1)} %constant_dynamic-slice_fusion), channel_id=1, source_target_pairs={{0,1},{1,0},{2,3},{3,2},{4,5},{5,4},{6,7},{7,6},{8,9},{9,8},{10,11... | collective-permute-start | bytes 6291464 | tf_op jit(solution)/shard_map/ppermute | solution.py:659
  441.1 55.2 %copy-start.9 = (f32[96,1024]{1,0:T(8,128)S(1)}, f32[96,1024]{1,0:T(8,128)}, u32[]{:S(2)}) copy-start(f32[96,1024]{1,0:T(8,128)} %get-tuple-element.36) | copy-start | bytes 1179652
  441.1 56.3 %copy-start.8 = (f32[96,1024]{1,0:T(8,128)S(1)}, f32[96,1024]{1,0:T(8,128)}, u32[]{:S(2)}) copy-start(f32[96,1024]{1,0:T(8,128)} %get-tuple-element.38) | copy-start | bytes 1179652
  441.1 160.8 %collective-permute-start = (bf16[1,1024,1024]{2,1,0:T(8,128)(2,1)}, bf16[1,1024,1024]{2,1,0:T(8,128)(2,1)}, u32[]{:S(2)}, u32[]{:S(2)}) collective-permute-start(bf16[1,1024,1024]{2,1,0:T(8,128)(2,1)} %constant_dynamic-slice_fusion.1), channel_id=1, source_target_pairs={{0,1},{1,0},{2,3},{3,2},{4,5},{5,4},{6,7},{7,6},{8,9},{9,8},{10,11... | collective-permute-start | bytes 6291464 | tf_op jit(solution)/shard_map/ppermute | solution.py:659
  499.4 100.8 %all-reduce.4.cloned.1.call-start = ((), (), s32[]{:S(2)}) async-start(), calls=%async_computation.2 | async-start | bytes 393216 | tf_op jit(solution)/shard_map/psum | solution.py:669
Sparse Core Ops, SparseCore 0:
  499.5 45.0 reduce-scatter.1
  547.7 52.4 all-reduce.3

commit v2 on v1

--- a/solution.py
+++ b/solution.py
@@ -44,17 +44,19 @@
     return jnp.stack([start, size], axis=-1)
 
 
-def attn_fwd_kernel(rows, win, x, w, b, pk, pv, segk, segq, qkv, ctx, lse, kx, vt):
+NP = 8
+
+
+def attn_fwd_kernel(rows, win, x, w, b, pk, pv, segk, segq, qkv, ctx, lse, vt):
     row = pl.program_id(0)
-    y = nn(x[0], w[0]) + b[0]
-    q = (y[:, :256].astype(bf16) * 0.125).astype(bf16)
-    qkv[0, 0, :, :256] = q
-    kv = y[:, 256:].astype(bf16)
-    qkv[0, 0, :, 256:] = kv
-    kx[:L] = kv[:, :256]
-    kx[L:] = pk[0]
-    vt[:, :L] = kv[:, 256:].T
-    vt[:, L:] = pv[0].T
+    for g in range(4):
+        y = nn(x[0], w[g]) + b[g]
+        q = (y[:, :256].astype(bf16) * 0.125).astype(bf16)
+        qkv[0, g, :, :256] = q
+        kv = y[:, 256:].astype(bf16)
+        qkv[0, g, :, 256:] = kv
+        vt[256 * g : 256 * g + 256, :L] = kv[:, 256:].T
+        vt[256 * g : 256 * g + 256, L:] = pv[g].T
 
     def tile(t, carry):
         start = win[row, t, 0]
@@ -65,23 +67,42 @@
         def run(n):
             W = n * BLK
             mask = segk[0, pl.ds(k0, W), :] == segq[0, :, pl.ds(q0, BLK)]
-            for p in range(2):
-                lanes = slice(128 * p, 128 * p + 128)
-                q2 = stack_heads(qkv[0, 0, pl.ds(q0, BLK), lanes])
-                s = nt(kx[pl.ds(k0, W), lanes], q2)
-                s = jnp.concatenate([jnp.where(mask, s[:, :128], NEG), jnp.where(mask, s[:, 128:], NEG)], axis=1)
-                sp = nt(kx[L : L + PRE, lanes], q2)
-                top = jnp.maximum(jnp.max(s, axis=0, keepdims=True), jnp.max(sp, axis=0, keepdims=True))
-                e = jnp.exp(s - top)
-                ep = jnp.exp(sp - top)
-                total = jnp.sum(e, axis=0, keepdims=True) + jnp.sum(ep, axis=0, keepdims=True)
-                o = nn(vt[lanes, pl.ds(k0, W)], e.astype(bf16)) + nn(vt[lanes, L : L + PRE], ep.astype(bf16))
-                o = o * (1.0 / total)
-                o = jnp.concatenate([o[:64, :128], o[64:, 128:]], axis=0)
-                ctx[0, pl.ds(q0, BLK), lanes] = o.T.astype(bf16)
-                lt = top + jnp.log(total)
-                lse[0, 0, 2 * p : 2 * p + 1, pl.ds(q0, BLK)] = lt[:, :128]
-                lse[0, 0, 2 * p + 1 : 2 * p + 2, pl.ds(q0, BLK)] = lt[:, 128:]
+
+            def batch(i, carry):
+                jobs = []
+                for j in range(NP):
+                    p = i * NP + j
+                    g, half = p // 2, j % 2
+                    lanes = slice(128 * half, 128 * half + 128)
+                    klanes = slice(256 + 128 * half, 384 + 128 * half)
+                    q2 = stack_heads(qkv[0, g, pl.ds(q0, BLK), lanes])
+                    jobs.append((p, g, half, nt(qkv[0, g, pl.ds(k0, W), klanes], q2), nt(pk[g, :PRE, lanes], q2)))
+                stage = []
+                for p, g, half, s, sp in jobs:
+                    s = jnp.concatenate([jnp.where(mask, s[:, :128], NEG), jnp.where(mask, s[:, 128:], NEG)], axis=1)
+                    top = jnp.maximum(jnp.max(s, axis=0, keepdims=True), jnp.max(sp, axis=0, keepdims=True))
+                    stage.append((s, sp, top))
+                probs = []
+                for s, sp, top in stage:
+                    e = jnp.exp(s - top)
+                    ep = jnp.exp(sp - top)
+                    total = jnp.sum(e, axis=0, keepdims=True) + jnp.sum(ep, axis=0, keepdims=True)
+                    probs.append((e.astype(bf16), ep.astype(bf16), total, top))
+                outs = []
+                for (p, g, half, _, _), (e, ep, total, top) in zip(jobs, probs):
+                    r0 = pl.multiple_of(p * 128, 128)
+                    outs.append(nn(vt[pl.ds(r0, 128), pl.ds(k0, W)], e) + nn(vt[pl.ds(r0, 128), L : L + PRE], ep))
+                for (p, g, half, _, _), (e, ep, total, top), o in zip(jobs, probs, outs):
+                    o = o * (1.0 / total)
+                    o = jnp.concatenate([o[:64, :128], o[64:, 128:]], axis=0)
+                    r0 = pl.multiple_of(p * 128, 128)
+                    ctx[0, pl.ds(q0, BLK), pl.ds(r0, 128)] = o.T.astype(bf16)
+                    lt = top + jnp.log(total)
+                    lse[0, g, 2 * half : 2 * half + 1, pl.ds(q0, BLK)] = lt[:, :128]
+                    lse[0, g, 2 * half + 1 : 2 * half + 2, pl.ds(q0, BLK)] = lt[:, 128:]
+                return carry
+
+            lax.fori_loop(0, 8 // NP, batch, 0)
 
         for n in CLASSES:
             pl.when(size == n)(functools.partial(run, n))
@@ -92,92 +113,105 @@
 
 def attn_fwd(rows, win, x, w, b, pk, pv, segk, segq):
     R = rows.shape[0]
-    row = lambda r, g, *_: (r, 0, 0)
-    grp = lambda r, g, *_: (g, 0, 0)
+    row = lambda r, *_: (r, 0, 0)
+    all_ = lambda r, *_: (0, 0, 0)
     return pl.pallas_call(
         attn_fwd_kernel,
         grid_spec=pltpu.PrefetchScalarGridSpec(
             num_scalar_prefetch=2,
-            grid=(R, 4),
+            grid=(R,),
             in_specs=[
-                pl.BlockSpec((1, L, D), lambda r, g, rows, win: (rows[r], 0, 0)),
-                pl.BlockSpec((1, D, 768), grp),
-                pl.BlockSpec((1, 1, 768), grp),
-                pl.BlockSpec((1, 128, 256), grp),
-                pl.BlockSpec((1, 128, 256), grp),
+                pl.BlockSpec((1, L, D), lambda r, rows, win: (rows[r], 0, 0)),
+                pl.BlockSpec((4, D, 768), all_),
+                pl.BlockSpec((4, 1, 768), all_),
+                pl.BlockSpec((4, 128, 256), all_),
+                pl.BlockSpec((4, 128, 256), all_),
                 pl.BlockSpec((1, L, 128), row),
                 pl.BlockSpec((1, 1, L), row),
             ],
             out_specs=[
-                pl.BlockSpec((1, 1, L, 768), lambda r, g, *_: (r, g, 0, 0)),
-                pl.BlockSpec((1, L, 256), lambda r, g, *_: (r, 0, g)),
-                pl.BlockSpec((1, 1, 4, L), lambda r, g, *_: (r, g, 0, 0)),
+                pl.BlockSpec((1, 4, L, 768), lambda r, *_: (r, 0, 0, 0)),
+                pl.BlockSpec((1, L, D), row),
+                pl.BlockSpec((1, 4, 4, L), lambda r, *_: (r, 0, 0, 0)),
             ],
-            scratch_shapes=[pltpu.VMEM((L + 128, 256), bf16), pltpu.VMEM((256, L + 128), bf16)],
+            scratch_shapes=[pltpu.VMEM((D, L + 128), bf16)],
         ),
         out_shape=[
             jax.ShapeDtypeStruct((R, 4, L, 768), bf16),
             jax.ShapeDtypeStruct((R, L, D), bf16),
             jax.ShapeDtypeStruct((R, 4, 4, L), f32),
         ],
-        compiler_params=pltpu.CompilerParams(vmem_limit_bytes=48 << 20),
+        compiler_params=pltpu.CompilerParams(vmem_limit_bytes=60 << 20),
         name="attn_fwd",
     )(rows, win, x, w, b, pk, pv, segk, segq)
 
 
-def attn_bwd_kernel(r, rows, win, qkv, ctx, gctx, lse, pk, pv, segk, segq, gfirst, w, *rest):
-    gin, pkg, pvg, dqt, dall, delta = rest[-6:]
-    row = r
-    g = pl.program_id(0)
-    prod = gctx[0].astype(f32) * ctx[0].astype(f32)
-    head = lax.broadcasted_iota(jnp.int32, (8, 256), 0)
-    lane = lax.broadcasted_iota(jnp.int32, (8, 256), 1)
-    pick = (lane // 64 == head).astype(f32)
-    delta[...] = lax.dot_general(
-        pick, prod, (((1,), (1,)), ((), ())), precision=lax.Precision.HIGHEST, preferred_element_type=f32
-    )
-
-    def block(kt, vt, mask, p, q0, W, first):
-        n = kt.shape[0]
-        lanes = slice(128 * p, 128 * p + 128)
-        k2 = stack_heads(kt)
-        v2 = stack_heads(vt)
-        qw = qkv[0, 0, pl.ds(q0, W), lanes]
-        dow = gctx[0, pl.ds(q0, W), lanes]
-        s = nt(k2, qw)
-        dp = nt(v2, dow)
-        ps, ds = [], []
-        for h in range(2):
-            lrow = lse[0, 0, 2 * p + h : 2 * p + h + 1, pl.ds(q0, W)]
-            drow = delta[2 * p + h : 2 * p + h + 1, pl.ds(q0, W)]
-            sh = s[h * n : h * n + n] - lrow
-            if mask is not None:
-                sh = jnp.where(mask, sh, NEG)
-            ph = jnp.exp(sh)
-            ps.append(ph.astype(bf16))
-            ds.append((ph * (dp[h * n : h * n + n] - drow)).astype(bf16))
-        pb = jnp.concatenate(ps, axis=0)
-        db = jnp.concatenate(ds, axis=0)
-        dv = nn(pb, dow)
-        dk = nn(db, qw)
-        part = nn(k2.T, db)
-        if first:
-            dqt[lanes, pl.ds(q0, W)] = part
-        else:
-            dqt[lanes, pl.ds(q0, W)] += part
+NB = 4
+
+
+def attn_bwd_kernel(row, rows, win, qkv, gctx, lse, delta, pk, pv, segk, segq, gfirst_h, w_h, *rest):
+    gin, own, pgrad, dqt, dall, gfirst, w, sem = rest[-8:]
+    late = [
+        pltpu.make_async_copy(gfirst_h.at[row], gfirst, sem.at[0]),
+        pltpu.make_async_copy(w_h, w, sem.at[1]),
+    ]
+    for c in late:
+        c.start()
+
+    def blocks(jobs, mask, q0, W, first):
+        n = jobs[0][3].shape[0]
+        stage = []
+        for p, g, half, kt, vt in jobs:
+            lanes = slice(128 * half, 128 * half + 128)
+            k2 = stack_heads(kt)
+            qw = qkv[0, g, pl.ds(q0, W), lanes]
+            dow = gctx[0, pl.ds(q0, W), pl.ds(pl.multiple_of(p * 128, 128), 128)]
+            stage.append((k2, qw, dow, nt(k2, qw), nt(stack_heads(vt), dow)))
+        probs = []
+        for (p, g, half, _, _), (k2, qw, dow, s, dp) in zip(jobs, stage):
+            ps, ds = [], []
+            for h in range(2):
+                r = 2 * half + h
+                sh = s[h * n : h * n + n] - lse[0, g, r : r + 1, pl.ds(q0, W)]
+                if mask is not None:
+                    sh = jnp.where(mask, sh, NEG)
+                ph = jnp.exp(sh)
+                ps.append(ph.astype(bf16))
+                ds.append((ph * (dp[h * n : h * n + n] - delta[0, g, r : r + 1, pl.ds(q0, W)])).astype(bf16))
+            probs.append((jnp.concatenate(ps, axis=0), jnp.concatenate(ds, axis=0)))
         lane = lax.broadcasted_iota(jnp.int32, (n, 128), 1)
-        return jnp.where(lane < 64, dk[:n], dk[n:]), jnp.where(lane < 64, dv[:n], dv[n:])
-
-    for p in range(2):
-        lanes = slice(128 * p, 128 * p + 128)
-        sk = jnp.zeros((PRE, 128), f32)
-        sv = jnp.zeros((PRE, 128), f32)
+        res = []
+        for (p, g, half, _, _), (k2, qw, dow, _, _), (pb, db) in zip(jobs, stage, probs):
+            dv = nn(pb, dow)
+            dk = nn(db, qw)
+            res.append((jnp.where(lane < 64, dk[:n], dk[n:]), jnp.where(lane < 64, dv[:n], dv[n:])))
+        for (p, g, half, _, _), (k2, _, _, _, _), (pb, db) in zip(jobs, stage, probs):
+            part = nn(k2.T, db)
+            r0 = pl.multiple_of(p * 128, 128)
+            if first:
+                dqt[pl.ds(r0, 128), pl.ds(q0, W)] = part
+            else:
+                dqt[pl.ds(r0, 128), pl.ds(q0, W)] += part
+        return res
+
+    def prefix(i, carry):
+        jobs = []
+        for j in range(NB):
+            p = i * NB + j
+            g, half = p // 2, j % 2
+            lanes = slice(128 * half, 128 * half + 128)
+            jobs.append((p, g, half, pk[g, :PRE, lanes], pv[g, :PRE, lanes]))
+        total = None
         for c in range(2):
-            dk, dv = block(pk[0, :PRE, lanes], pv[0, :PRE, lanes], None, p, c * 512, 512, True)
-            sk = sk + dk
-            sv = sv + dv
-        pkg[:, lanes] = sk
-        pvg[:, lanes] = sv
+            part = blocks(jobs, None, c * 512, 512, True)
+            total = part if total is None else [(a + c_, b + d) for (a, b), (c_, d) in zip(total, part)]
+        for (p, g, half, _, _), (dk, dv) in zip(jobs, total):
+            cols = pl.ds(pl.multiple_of(p * 128, 128), 128)
+            pgrad[0, :, cols] = dk
+            pgrad[1, :, cols] = dv
+        return carry
+
+    lax.fori_loop(0, 8 // NB, prefix, 0)
 
     def tile(t, carry):
         start = win[row, t, 0]
@@ -190,77 +224,86 @@
             sk = segk[0, pl.ds(k0, BLK), :]
             sq = segq[0, :, pl.ds(q0, W)]
             mask = jnp.concatenate([sk] * n, axis=1) == sq
-            for p in range(2):
-                kt = qkv[0, 0, pl.ds(k0, BLK), 256 + 128 * p : 384 + 128 * p]
-                vt = qkv[0, 0, pl.ds(k0, BLK), 512 + 128 * p : 640 + 128 * p]
-                dk, dv = block(kt, vt, mask, p, q0, W, False)
-                dall[g, pl.ds(k0, BLK), 256 + 128 * p : 384 + 128 * p] = dk.astype(bf16)
-                dall[g, pl.ds(k0, BLK), 512 + 128 * p : 640 + 128 * p] = dv.astype(bf16)
+
+            def batch(i, carry):
+                jobs = []
+                for j in range(NB):
+                    p = i * NB + j
+                    g, half = p // 2, j % 2
+                    kt = qkv[0, g, pl.ds(k0, BLK), 256 + 128 * half : 384 + 128 * half]
+                    vt = qkv[0, g, pl.ds(k0, BLK), 512 + 128 * half : 640 + 128 * half]
+                    jobs.append((p, g, half, kt, vt))
+                for (p, g, half, _, _), (dk, dv) in zip(jobs, blocks(jobs, mask, q0, W, False)):
+                    dall[g, pl.ds(k0, BLK), 256 + 128 * half : 384 + 128 * half] = dk.astype(bf16)
+                    dall[g, pl.ds(k0, BLK), 512 + 128 * half : 640 + 128 * half] = dv.astype(bf16)
+                return carry
+
+            lax.fori_loop(0, 8 // NB, batch, 0)
 
         for n in CLASSES:
             pl.when(size == n)(functools.partial(run, n))
         return carry
 
     lax.fori_loop(0, L // BLK, tile, 0)
-    dall[g, :, :256] = (dqt[...].T * 0.125).astype(bf16)
-
-    @pl.when(g == 3)
-    def _():
-        def cols(c, carry):
-            c0 = pl.multiple_of(c * 256, 256)
-            acc = gfirst[0, :, pl.ds(c0, 256)].astype(f32)
-            for i in range(4):
-                acc = acc + nt(dall[i], w[i, pl.ds(c0, 256), :])
-            gin[0, :, pl.ds(c0, 256)] = acc.astype(bf16)
-            return carry
-
-        lax.fori_loop(0, 4, cols, 0)
-
-
-def attn_bwd(r, rows, win, qkv, ctx, gctx, lse, pk, pv, segk, segq, gfirst, w, into=None):
-    row = lambda g, *_: (r, 0, 0)
-    grp = lambda g, *_: (g, 0, 0)
-    rg = lambda g, *_: (r, g, 0, 0)
-    cg = lambda g, *_: (r, 0, g)
+    for c in late:
+        c.wait()
+    for g in range(4):
+        dall[g, :, :256] = (dqt[256 * g : 256 * g + 256, :].T * 0.125).astype(bf16)
+    for c in range(2):
+        cols = slice(512 * c, 512 * c + 512)
+        acc = gfirst[:, cols].astype(f32)
+        for i in range(4):
+            acc = acc + nt(dall[i], w[i, cols, :])
+        low = acc.astype(bf16)
+        gin[0, :, cols] = low
+        own[:, cols] = low
+
+
+def attn_bwd(r, rows, win, qkv, gctx, lse, delta, pk, pv, segk, segq, gfirst, w, into=None):
+    row = lambda i, *_: (r, 0, 0)
+    row4 = lambda i, *_: (r, 0, 0, 0)
+    all_ = lambda i, *_: (0, 0, 0)
     extra = [] if into is None else [into]
     return pl.pallas_call(
         functools.partial(attn_bwd_kernel, r),
         grid_spec=pltpu.PrefetchScalarGridSpec(
             num_scalar_prefetch=2,
-            grid=(4,),
+            grid=(1,),
             in_specs=[
-                pl.BlockSpec((1, 1, L, 768), rg),
-                pl.BlockSpec((1, L, 256), cg),
-                pl.BlockSpec((1, L, 256), cg),
-                pl.BlockSpec((1, 1, 4, L), rg),
-                pl.BlockSpec((1, 128, 256), grp),
-                pl.BlockSpec((1, 128, 256), grp),
+                pl.BlockSpec((1, 4, L, 768), row4),
+                pl.BlockSpec((1, L, D), row),
+                pl.BlockSpec((1, 4, 4, L), row4),
+                pl.BlockSpec((1, 4, 4, L), row4),
+                pl.BlockSpec((4, 128, 256), all_),
+                pl.BlockSpec((4, 128, 256), all_),
                 pl.BlockSpec((1, L, 128), row),
                 pl.BlockSpec((1, 1, L), row),
-                pl.BlockSpec((1, L, D), row),
-                pl.BlockSpec((4, D, 768), lambda g, *_: (0, 0, 0)),
+                pl.BlockSpec(memory_space=pl.ANY),
+                pl.BlockSpec(memory_space=pl.ANY),
             ]
             + [pl.BlockSpec(memory_space=pl.ANY) for _ in extra],
             out_specs=[
-                pl.BlockSpec((1, L, D), lambda g, rows, win: (rows[r], 0, 0)),
-                pl.BlockSpec((PRE, 256), lambda g, *_: (0, g)),
-                pl.BlockSpec((PRE, 256), lambda g, *_: (0, g)),
+                pl.BlockSpec((1, L, D), lambda i, rows, win: (rows[r], 0, 0)),
+                pl.BlockSpec((L, D), lambda i, *_: (0, 0)),
+                pl.BlockSpec((2, PRE, D), all_),
             ],
             scratch_shapes=[
-                pltpu.VMEM((256, L), f32),
+                pltpu.VMEM((D, L), f32),
                 pltpu.VMEM((4, L, 768), bf16),
-                pltpu.VMEM((8, L), f32),
+                pltpu.VMEM((L, D), bf16),
+                pltpu.VMEM((4, D, 768), bf16),
+                pltpu.SemaphoreType.DMA((2,)),
             ],
         ),
         out_shape=[
             jax.ShapeDtypeStruct((3, L, D), bf16),
-            jax.ShapeDtypeStruct((PRE, D), f32),
-            jax.ShapeDtypeStruct((PRE, D), f32),
+            jax.ShapeDtypeStruct((L, D), bf16),
+            jax.ShapeDtypeStruct((2, PRE, D), f32),
         ],
         input_output_aliases={12: 0} if extra else {},
-        compiler_params=pltpu.CompilerParams(vmem_limit_bytes=56 << 20),
+        compiler_params=pltpu.CompilerParams(vmem_limit_bytes=60 << 20),
         name="attn_bwd",
-    )(rows, win, qkv, ctx, gctx, lse, pk, pv, segk, segq, gfirst, w, *extra)
+    )(rows, win, qkv, gctx, lse, delta, pk, pv, segk, segq, gfirst, w, *extra)
 
 
 HC = 512
@@ -293,7 +336,7 @@
 RC = 512
 
 
-def tokens_kernel(rows, ctx, x, cot, wo, win, wout, bo, g1, s1, bi, b2, g2, s2, out, gf, gc, xhat, zbuf, low, act, gp, rs, vb):
+def tokens_kernel(rows, ctx, x, cot, wo, win, wout, bo, g1, s1, bi, b2, g2, s2, out, own, gf, gc, delta, xhat, zbuf, low, act, gp, rs, vb):
     M = TM
 
     def dot_cols(i, carry):
@@ -338,7 +381,9 @@
     def ln2(i, carry):
         r0 = pl.multiple_of(i * RC, RC)
         n, r = norm_stats(zbuf[pl.ds(r0, RC), :] + b2[...])
-        out[pl.ds(r0, RC), :] = (n * g2[...] + s2[...]).astype(bf16)
+        result = (n * g2[...] + s2[...]).astype(bf16)
+        out[pl.ds(r0, RC), :] = result
+        own[pl.ds(r0, RC), :] = result
         g = cot[pl.ds(r0, RC), :].astype(f32) * g2[...]
         m1 = jnp.mean(g, axis=1, keepdims=True)
         m2 = jnp.mean(g * n, axis=1, keepdims=True)
@@ -383,7 +428,15 @@
 
     def gcols(i, carry):
         c0 = pl.multiple_of(i * 256, 256)
-        gc[:, pl.ds(c0, 256)] = nt(gf[...], wo[pl.ds(c0, 256), :]).astype(bf16)
+        part = nt(gf[...], wo[pl.ds(c0, 256), :]).astype(bf16)
+        gc[:, pl.ds(c0, 256)] = part
+        prod = part.astype(f32) * ctx[:, pl.ds(c0, 256)].astype(f32)
+        high = prod.astype(bf16)
+        rest = (prod - high.astype(f32)).astype(bf16)
+        head = lax.broadcasted_iota(jnp.int32, (16, 256), 0)
+        lane = lax.broadcasted_iota(jnp.int32, (16, 256), 1)
+        pick = jnp.where(lane // 64 == head, 1.0, 0.0).astype(bf16)
+        delta[i] = (nt(pick, high) + nt(pick, rest))[:4]
         return carry
 
     lax.fori_loop(0, 4, gcols, 0, unroll=4)
@@ -402,7 +455,7 @@
             num_scalar_prefetch=1,
             grid=(R * per,),
             in_specs=[own, pick, pick] + [whole(a) for a in consts],
-            out_specs=[pick, own, own],
+            out_specs=[pick, own, own, own, pl.BlockSpec((None, 4, 4, TM), lambda i, rows: (i // per, 0, 0, i % per))],
             scratch_shapes=[
                 pltpu.VMEM((TM, D), f32),
                 pltpu.VMEM((TM, D), f32),
@@ -417,6 +470,8 @@
             jax.ShapeDtypeStruct((3, L, D), bf16),
             jax.ShapeDtypeStruct((R, L, D), bf16),
             jax.ShapeDtypeStruct((R, L, D), bf16),
+            jax.ShapeDtypeStruct((R, L, D), bf16),
+            jax.ShapeDtypeStruct((R, 4, 4, L), f32),
         ],
         compiler_params=pltpu.CompilerParams(vmem_limit_bytes=60 << 20),
         name="tokens",
@@ -624,6 +679,76 @@
     )
 
 
+def total_kernel(uniq, shared, other, key, value, mine, half, slots, ssem, rsem):
+    d = lax.axis_index("dp")
+    z = lax.axis_index("prefix")
+    core, chip = d % 2, d // 2
+    xx, yy = chip % 2, chip // 2
+    dc = d + 1 - 2 * core
+    peers = [((d + 2 - 4 * xx), chip + 1 - 2 * xx), ((d + 4 - 8 * yy), chip + 2 - 4 * yy)]
+    peers.append((peers[0][0] + peers[1][0] - d, 3 - chip))
+    bar = pltpu.get_barrier_semaphore()
+    for dd in (dc, *(p for p, _ in peers)):
+        pl.semaphore_signal(bar, inc=1, device_id=(dd, z), device_id_type=pl.DeviceIdType.MESH)
+    n = key.shape[0]
+    r0 = pl.multiple_of(z * n, 8)
+    mine[...] = uniq[:, pl.ds(r0, n), :] + shared[:, pl.ds(r0, n), :] + other[...]
+    pl.semaphore_wait(bar, 4)
+
+    def send(src, dst, i, dd):
+        return pltpu.make_async_remote_copy(
+            src_ref=src, dst_ref=dst, send_sem=ssem.at[i], recv_sem=rsem.at[i],
+            device_id=(dd, z), device_id_type=pl.DeviceIdType.MESH,
+        )
+
+    first = send(mine.at[1 - core], half, 0, dc)
+    first.start()
+    first.wait()
+    slots[chip] = mine[core] + half[...]
+    copies = [send(slots.at[chip], slots.at[chip], 1 + i, dd) for i, (dd, _) in enumerate(peers)]
+    for c in copies:
+        c.start()
+    for c in copies:
+        c.wait()
+    total = (slots[0] + slots[1]) + (slots[2] + slots[3])
+
+    @pl.when(core == 0)
+    def _():
+        key[...] = total
+        last = send(key, key, 4, dc)
+        last.start()
+        last.wait_send()
+        send(value, value, 5, dc).wait_recv()
+
+    @pl.when(core == 1)
+    def _():
+        value[...] = total
+        last = send(value, value, 5, dc)
+        last.start()
+        last.wait_send()
+        send(key, key, 4, dc).wait_recv()
+
+
+def total_grads(uniq, shared, other):
+    n = other.shape[1]
+    vmem = pl.BlockSpec(memory_space=pltpu.VMEM)
+    return pl.pallas_call(
+        total_kernel,
+        in_specs=[vmem] * 3,
+        out_specs=[vmem] * 2,
+        out_shape=[jax.ShapeDtypeStruct((n, D), f32)] * 2,
+        scratch_shapes=[
+            pltpu.VMEM((2, n, D), f32),
+            pltpu.VMEM((n, D), f32),
+            pltpu.VMEM((4, n, D), f32),
+            pltpu.SemaphoreType.DMA((6,)),
+            pltpu.SemaphoreType.DMA((6,)),
+        ],
+        compiler_params=pltpu.CompilerParams(collective_id=1, has_side_effects=True),
+        name="total_grads",
+    )(uniq, shared, other)
+
+
 def body(
     hidden_in, cotangent, segment_ids, key_mask, prefix_keys, prefix_values,
     w_query, b_query, w_key, b_key, w_value, b_value, w_attn_out, b_attn_out, gain_attn, shift_attn,
@@ -634,7 +759,8 @@
     rows = jnp.stack([2 * side, jnp.ones_like(side)]).astype(jnp.int32)
     pre = jnp.concatenate([prefix_keys, prefix_values], axis=0)
     vec = jnp.concatenate([b_query, b_key, b_value, b_ffn_in, jnp.zeros((256,), f32)]).reshape(8, 256)
-    whole = gather if lax.axis_size("dp") == 8 and lax.axis_size("prefix") == 4 else gather_plain
+    small = lax.axis_size("dp") == 8 and lax.axis_size("prefix") == 4
+    whole = gather if small else gather_plain
     pre, vec, w_qkv, w_out, w_up, w_down = whole(
         pre, vec, w_query, w_key, w_value, w_attn_out, w_ffn_in, w_ffn_out
     )
@@ -651,23 +777,26 @@
     segq = seg[:, None, :]
 
     qkv, ctx, lse = attn_fwd(rows, win, hidden_in, w_qkv, b_qkv, pk, pv, segk, segq)
-    out, gfirst, gctx = tokens(
+    out, out_own, gfirst, gctx, delta = tokens(
         rows, ctx, hidden_in, cotangent, w_out, w_up, w_down, line(b_attn_out), line(gain_attn), line(shift_attn),
         b_up, line(b_ffn_out), line(gain_ffn), line(shift_ffn),
     )
     pairs = [(i, i + 1 - 2 * (i % 2)) for i in range(lax.axis_size("prefix"))]
-    swap = lambda v: lax.ppermute(lax.dynamic_slice_in_dim(v, rows[0], 1, 0), "prefix", pairs)
-    put = lambda v, r: lax.dynamic_update_slice_in_dim(v, r, 2 - rows[0], 0)
-    out_other = swap(out)
-    args = (rows, win, qkv, ctx, gctx, lse, pk, pv, segk, segq, gfirst, w_qkv)
-    gin, ku, vu = attn_bwd(0, *args)
-    gin_other = swap(gin)
-    gin, ks, vs = attn_bwd(1, *args, into=gin)
-    unique = (z < 2).astype(f32)
-    shared = (z == 0).astype(f32)
-    both = jnp.stack([ku * unique + ks * shared, vu * unique + vs * shared])
-    both = lax.psum(lax.psum_scatter(both, "prefix", scatter_dimension=1, tiled=True), "dp")
-    return put(out, out_other), put(gin, gin_other), both[0], both[1]
+    swap = lambda v: lax.ppermute(v, "prefix", pairs)
+    put = lambda v, r: lax.dynamic_update_slice_in_dim(v, r[None], 2 - rows[0], 0)
+    out_other = swap(out_own[0])
+    args = (rows, win, qkv, gctx, lse, delta, pk, pv, segk, segq, gfirst, w_qkv)
+    gin, gin_own, uniq = attn_bwd(0, *args)
+    gin_other = swap(gin_own)
+    n = PRE // lax.axis_size("prefix")
+    other = swap(lax.dynamic_slice_in_dim(uniq, (z + 1 - 2 * side) * n, n, 1))
+    gin, _, shared = attn_bwd(1, *args, into=gin)
+    if small:
+        keys, values = total_grads(uniq, shared, other)
+    else:
+        mine = lax.dynamic_slice_in_dim(uniq + shared, z * n, n, 1) + other
+        keys, values = lax.psum(mine, "dp")
+    return put(out, out_other), put(gin, gin_other), keys, values
 
 
 def solution(mesh):

time: 607 us -> 478 us (0.79); the launches traced: 613 us -> 472 us
  waiting for transfers between devices: 101 us -> 0.01 us
  Pallas kernels: 460 us -> 443 us
  between operations: 14.5 us -> 1.09 us
  starting transfers between devices: 9.49 us -> 2.13 us
    psum x1 -> x0, waiting for transfers between devices: 55.6 us -> none  [body(): lax.psum(lax.psum_scatter(both, 'prefix', scatter_dimension=1, tiled=True...]
    reduce_scatter x1 -> x0, waiting for transfers between devices: 45.2 us -> none  [body(): lax.psum_scatter(both, 'prefix', scatter_dimension=1, tiled=True)]
    pallas_call x1, Pallas kernels: 89.3 us -> 60.4 us  [attn_fwd(): pl.pallas_call(attn_fwd_kernel, grid_spec=pltpu.PrefetchScalarGridSpec(nu...]
    pallas_call x0 -> x1, Pallas kernels: none -> 16.9 us  [total_grads(): pl.pallas_call(total_kernel, in_specs=[vmem] * 3, out_specs=[vmem] * 2, o...]
    pallas_call x2, Pallas kernels: 105 us -> 90.4 us  [attn_bwd(): pl.pallas_call(functools.partial(attn_bwd_kernel, r), grid_spec=pltpu.Pre...]
    pallas_call x1, Pallas kernels: 122 us -> 132 us  [tokens(): pl.pallas_call(tokens_kernel, grid_spec=pltpu.PrefetchScalarGridSpec(num_...]
    ppermute x2 -> x3, starting transfers between devices: 9.41 us -> 2.13 us  [body(): swap = lambda v: lax.ppermute(v, 'prefix', pairs)]
  transfers between devices with their start and end apart: 4 -> 3, of which waited for: 2 -> 0; matrix products, arithmetic and copies ran while one was open for 2% -> 1% of each run, Pallas kernels for 9% -> 23%
where the time goes in v2:
time: 478 us; the launch traced here: 472 us
  Pallas kernels  443 us (93%)
  local copies, waits for them, and re-layouts  21.8 us (5%)
    pallas_call x1, Pallas kernels, gather(): pl.pallas_call(gather_kernel, in_specs=[any_] * 8, out_specs=[any_] * 6,...  144 us
    pallas_call x1, Pallas kernels, tokens(): pl.pallas_call(tokens_kernel, grid_spec=pltpu.PrefetchScalarGridSpec(num_...  132 us
    pallas_call x2, Pallas kernels, attn_bwd(): pl.pallas_call(functools.partial(attn_bwd_kernel, r), grid_spec=pltpu.Pre...  90.4 us
    pallas_call x1, Pallas kernels, attn_fwd(): pl.pallas_call(attn_fwd_kernel, grid_spec=pltpu.PrefetchScalarGridSpec(nu...  60.4 us
    pallas_call x1, Pallas kernels, total_grads(): pl.pallas_call(total_kernel, in_specs=[vmem] * 3, out_specs=[vmem] * 2, o...  16.9 us
  transfers between devices with their start and end apart: 3, of which 0 were waited for; matrix products, arithmetic and copies ran while one was open for 1% of the time, Pallas kernels for 23%

profile of v2, /device:TPU:0, one launch (start us, length us, event | category | flops | bytes accessed | tf_op | source)
XLA Modules:
  0.0 472.2 jit_solution(4362366543569895200)
XLA Ops:
  0.7 0.9 broadcast_select_fusion
  1.6 0.1 slice.43
  1.7 0.1 slice.42
  1.8 0.6 broadcast_in_dim.35.segq
  2.4 0.7 constant_dynamic-update-slice_fusion.4
  3.0 0.7 constant_dynamic-update-slice_fusion.3
  3.7 0.7 constant_dynamic-update-slice_fusion.2
  4.4 0.7 constant_dynamic-update-slice_fusion.1
  5.1 0.6 reshape.224.vec_s
  5.7 1.5 pad_maximum_fusion.pre_s
  7.2 143.7 %gather.1 = (bf16[4,48,1024]{2,1,0:T(8,128)(2,1)}, f32[4,8,256]{2,1,0:T(8,128)}, bf16[4,1024,768]{2,1,0:T(8,128)(2,1)}, bf16[1024,1024]{1,0:T(8,128)(2,1)}, bf16...) custom-call(bf16[48,1024]{1,0:T(8,128)(2,1)} %pad_maximum_fusion.pre_s, f32[8,256]{1,0:T(8,128)} %reshape.224.vec_s, ...), custom_call_target="tpu_custom_call" | custom-call | tf_op jit(solution)/shard_map/gather/pallas_call | solution.py:646
  150.9 0.8 slice.50
  151.7 0.8 slice.44
  152.4 0.2 convert_reduce_fusion.1
  152.7 0.1 copy.58
  152.8 0.1 copy.54
  152.8 1.1 fusion.5
  153.9 0.1 reshape.227
  154.1 0.6 reshape.235.b
  154.7 0.6 reshape.231.bi
  155.3 0.1 reshape.226
  155.5 0.7 pad.8.pv
  156.2 0.7 pad.7.pk
  156.9 0.6 pad_add_fusion.2.rows
  157.6 0.7 pad_add_fusion.1.win
  158.2 1.3 broadcast_in_dim.34.segk
  159.5 60.4 %attn_fwd.1 = (bf16[2,4,1024,768]{3,2,1,0:T(8,128)(2,1)}, bf16[2,1024,1024]{2,1,0:T(8,128)(2,1)}, f32[2,4,4,1024]{3,2,1,0:T(4,128)}) custom-call(s32[2]{0:T(128)} %pad_add_fusion.2.rows, s32[2,8,2]{2,1,0:T(8,128)} %pad_add_fusion.1.win, bf16[3,1024,1024]{2,1,0:T(8,128)(2,1)} %x.7, bf16[4,1024,768]{2,1,0:T(8,128)(2,1)} %get-tuple-element.25.w.w_h, ...), custom_call_target="tpu_custom_call" | custom-call | tf_op jit(solution)/shard_map/attn_fwd/pallas_call | solution.py:118
  220.0 131.8 %tokens.1 = (bf16[3,1024,1024]{2,1,0:T(8,128)(2,1)}, bf16[2,1024,1024]{2,1,0:T(8,128)(2,1)}, bf16[2,1024,1024]{2,1,0:T(8,128)(2,1)}, bf16[2,1024,1024]{2,1,0:T(8,128)(2,1)}, f32[2,4,4,1024]{3,2,1,0:T(4,128)}) custom-call(s32[2]{0:T(128)} %pad_add_fusion.2.rows, bf16[2,1024,1024]{2,1,0:T(8,128)(2,1)} %get-tuple-element.28.ctx, bf16[3,1024,1024]{2,1,0:T(8,128)(2,1)} %x.7, ...), custom_call_target="tpu_custom_call" | custom-call | tf_op jit(solution)/shard_map/tokens/pallas_call | solution.py:452
  351.8 3.1 slice_bitcast_fusion
  354.9 0.0 collective-permute-start
  354.9 45.0 %attn_bwd.2 = (bf16[3,1024,1024]{2,1,0:T(8,128)(2,1)}, bf16[1024,1024]{1,0:T(8,128)(2,1)}, f32[2,96,1024]{2,1,0:T(8,128)}) custom-call(s32[2]{0:T(128)} %pad_add_fusion.2.rows, s32[2,8,2]{2,1,0:T(8,128)} %pad_add_fusion.1.win, bf16[2,4,1024,768]{3,2,1,0:T(8,128)(2,1)} %get-tuple-element.34.qkv, bf16[2,1024,1024]{2,1,0:T(8,128)(2,1)} %get-tuple-element.35.gctx, ...), custom_call_target="tpu_custom_call" | custom-call | tf_op jit(solution)/shard_map/attn_bwd/pallas_call | solution.py:267
  399.9 0.1 collective-permute-start.1
  400.0 0.9 constant_dynamic-slice_fusion
  401.0 2.1 collective-permute-start.2
  403.0 45.4 %attn_bwd.3 = (bf16[3,1024,1024]{2,1,0:T(8,128)(2,1)}, bf16[1024,1024]{1,0:T(8,128)(2,1)}, f32[2,96,1024]{2,1,0:T(8,128)}) custom-call(s32[2]{0:T(128)} %pad_add_fusion.2.rows, s32[2,8,2]{2,1,0:T(8,128)} %pad_add_fusion.1.win, bf16[2,4,1024,768]{3,2,1,0:T(8,128)(2,1)} %get-tuple-element.34.qkv, ...), custom_call_target="tpu_custom_call", output_to_operand_aliasing={{0}: (12, {})} | custom-call | tf_op jit(solution)/shard_map/attn_bwd/pallas_call | solution.py:267
  448.4 0.0 collective-permute-done.2.other
  448.4 0.0 copy-start
  448.5 0.7 copy-done
  449.1 16.9 %total_grads.1 = (f32[24,1024]{1,0:T(8,128)}, f32[24,1024]{1,0:T(8,128)}) custom-call(f32[2,96,1024]{2,1,0:T(8,128)} %get-tuple-element.42.uniq, f32[2,96,1024]{2,1,0:T(8,128)} %get-tuple-element.43.shared, f32[2,24,1024]{2,1,0:T(8,128)} %copy-done), custom_call_target="tpu_custom_call" | custom-call | tf_op jit(solution)/shard_map/total_grads/pallas_call | solution.py:735
  466.0 0.0 copy-start.2
  466.0 0.0 copy-start.1
  466.0 0.0 collective-permute-done
  466.0 1.5 bitcast_dynamic-update-slice_fusion.1
  467.5 0.0 collective-permute-done.1
  467.5 3.1 bitcast_dynamic-update-slice_fusion
  470.6 0.0 copy-done.2
  470.6 0.6 copy.79
  471.3 0.0 copy-done.1
  471.3 0.6 copy.80
  (7 shorter events, 0.1 us)
Async XLA Ops:
  354.9 111.1 %collective-permute-start = (bf16[1024,1024]{1,0:T(8,128)(2,1)}, bf16[1024,1024]{1,0:T(8,128)(2,1)S(1)}, u32[]{:S(2)}, u32[]{:S(2)}) collective-permute-start(bf16[1024,1024]{1,0:T(8,128)(2,1)} %slice_bitcast_fusion), channel_id=1, source_target_pairs={{0,1},{1,0},{2,3},{3,2},{4,5},{5,4},{6,7},{7,6},{8,9},{9,8},{10,11... | collective-permute-start | bytes 6291464 | tf_op jit(solution)/shard_map/ppermute | solution.py:785
  399.9 67.6 %collective-permute-start.1 = (bf16[1024,1024]{1,0:T(8,128)(2,1)}, bf16[1024,1024]{1,0:T(8,128)(2,1)}, u32[]{:S(2)}, u32[]{:S(2)}) collective-permute-start(bf16[1024,1024]{1,0:T(8,128)(2,1)} %get-tuple-element.41), channel_id=1, source_target_pairs={{0,1},{1,0},{2,3},{3,2},{4,5},{5,4},{6,7},{7,6},{8,9},{9,8},{10,11... | collective-permute-start | bytes 6291464 | tf_op jit(solution)/shard_map/ppermute | solution.py:785
  401.0 47.5 %collective-permute-start.2 = (f32[2,24,1024]{2,1,0:T(8,128)S(1)}, f32[2,24,1024]{2,1,0:T(8,128)S(1)}, u32[]{:S(2)}, u32[]{:S(2)}) collective-permute-start(f32[2,24,1024]{2,1,0:T(8,128)S(1)} %constant_dynamic-slice_fusion), channel_id=1, source_target_pairs={{0,1},{1,0},{2,3},{3,2},{4,5},{5,4},{6,7},{7,6},{8,9},{9,8},{10,11... | collective-permute-start | bytes 589832 | tf_op jit(solution)/shard_map/ppermute | solution.py:785
  448.4 0.7 copy-start
  466.0 4.6 copy-start.2
  466.0 5.2 %copy-start.1 = (f32[24,1024]{1,0:T(8,128)S(1)}, f32[24,1024]{1,0:T(8,128)}, u32[]{:S(2)}) copy-start(f32[24,1024]{1,0:T(8,128)} %get-tuple-element.67) | copy-start | bytes 294916
